TPU v7x, 256 devices: a whole 4x4x8 slice. The times are simulated.
256 devices in a mesh: seq: 128 (over y, z_lo, x, core), ch: 2 (over z_hi).
Axes of the slice: x: 4, y: 4, z: 8 (z_hi: 2, z_lo: 4; z = z_hi * 4 + z_lo), core: 2. Of those that a mesh axis runs over, the one named last changes fastest.
Arguments:
- signal: bfloat16 [524288, 1024], P('seq', 'ch'), may hold values from -6 to 6
- twiddle: float32 [512, 1024], P('seq'), may hold values from -4 to 4
- row_factor: bfloat16 [1024, 1024], replicated, may hold values from -0.1875 to 0.1875
- col_factor: bfloat16 [512, 512], replicated, may hold values from -0.25 to 0.25
- block_mix: bfloat16 [64, 16, 16], P('ch'), may hold values from -1.5 to 1.5
- spread_mix: bfloat16 [16, 64, 64], replicated, may hold values from -0.75 to 0.75
- gate_scale: float32 [1024], P('ch'), may hold values from 0.5 to 2
Outputs:
- output: bfloat16 [524288, 1024], P('seq', 'ch')
All inputs are finite; a program needn't handle non-finite values.
Results may differ from a plain program's by a relative error of at most 0.0056.
Values may be sent and summed in bfloat16 or wider, within the bound.
A program may use at most 128 MiB of HBM per device.

v0:
```python
import jax
import jax.numpy as jnp
from jax import lax
from jax.sharding import PartitionSpec as P


def mix_columns(piece, col_factor, block_dense):
    mixed_cols = jnp.einsum(
        "im,iokc->mokc", col_factor, piece, preferred_element_type=jnp.float32
    ).astype(jnp.bfloat16)
    local_width = block_dense.shape[0]
    blocked = jnp.dot(
        mixed_cols.reshape(-1, local_width), block_dense, preferred_element_type=jnp.float32
    )
    return blocked.astype(jnp.bfloat16).reshape(mixed_cols.shape)


def restore_order(segmented, col_factor, block_dense):
    blocked = mix_columns(
        lax.all_to_all(segmented, "seq", split_axis=1, concat_axis=0, tiled=True),
        col_factor,
        block_dense,
    )
    arrived = lax.all_to_all(blocked, "seq", split_axis=0, concat_axis=1, tiled=True)
    return arrived.reshape(-1, arrived.shape[-1])


def send_back(spread_half):
    return lax.all_to_all(spread_half, "ch", split_axis=1, concat_axis=0, tiled=True)


def dense_blocks(block_weights):
    groups_count = block_weights.shape[0]
    block_width = block_weights.shape[1]
    group_mask = jnp.eye(groups_count, dtype=jnp.bfloat16)
    dense = block_weights[:, :, None, :] * group_mask[:, None, :, None]
    return dense.reshape(groups_count * block_width, groups_count * block_width)


def per_device(signal, twiddle, row_factor, col_factor, block_mix, spread_mix, gate_scale):
    seq_count = lax.axis_size("seq")
    row_count = twiddle.shape[0]
    col_count = twiddle.shape[1]
    local_width = signal.shape[1]
    block_width = block_mix.shape[1]
    groups_all = spread_mix.shape[1]
    lattice = signal.reshape(row_count, col_count, local_width)
    mixed_rows = jnp.einsum("ijc,jk->ikc", lattice, row_factor, preferred_element_type=jnp.float32)
    mixed_rows = (mixed_rows * twiddle[:, :, None]).astype(jnp.bfloat16)
    segmented = mixed_rows.reshape(row_count, seq_count, col_count // seq_count, local_width)
    block_dense = dense_blocks(block_mix)
    inner_mask = jnp.eye(block_width, dtype=jnp.bfloat16)
    spread_dense = spread_mix.transpose(1, 0, 2)[:, :, :, None] * inner_mask[None, :, None, :]
    spread_dense = spread_dense.reshape(groups_all * block_width, groups_all * block_width)
    blocked_all = restore_order(segmented, col_factor, block_dense)
    regrouped = lax.all_to_all(blocked_all, "ch", split_axis=0, concat_axis=1, tiled=True)
    spread_half = jnp.dot(regrouped, spread_dense, preferred_element_type=jnp.float32).astype(
        jnp.bfloat16
    )
    spread = send_back(spread_half)
    signal32 = signal.astype(jnp.float32)
    gated = jax.nn.silu(gate_scale[None, :] * signal32) * spread.astype(jnp.float32)
    return (signal32 + gated).astype(jnp.bfloat16)


def solution(mesh):
    placed = (P("seq", "ch"), P("seq", None), P(), P(), P("ch", None, None), P(), P("ch"))
    return jax.shard_map(
        per_device, mesh=mesh, in_specs=placed, out_specs=P("seq", "ch"), check_vma=False
    )
```

profile of v0, /device:TPU:38, one launch (start us, length us, event | category | flops | bytes accessed | tf_op | source)
XLA Modules:
  0.0 466.3 jit_solution(11890259482261475881)
XLA Ops:
  0.0 0.0 copy-start
  0.0 1.6 copy-done
  1.6 7.0 %fusion.8 = bf16[4,128,8,512]{3,2,1,0:T(8,128)(2,1)S(1)} fusion(f32[4,1024]{1,0:T(4,128)} %param.8, bf16[4,1024,512]{2,1,0:T(8,128)(2,1)} %bitcast.55, bf16[1024,1024]{1,0:T(8,128)(2,1)S(1)} %copy-done), kind=kOutput, calls=%fused_computation.14 | convolution fusion | flops 4299161600 | bytes 10502144 | tf_op jit(solution)/shard_map/ijc,jk->ikc/dot_general | solution.py:48
  8.6 2.6 copy.32
  11.2 0.0 copy-start.3
  11.2 13.0 %all-to-all-start = ((bf16[4,128,8,512]{3,2,0,1:T(8,128)(2,1)}), bf16[4,128,8,512]{3,2,0,1:T(8,128)(2,1)}, u32[]{:S(2)}, u32[]{:S(2)}) async-start(bf16[4,128,8,512]{3,2,0,1:T(8,128)(2,1)} %copy.32), calls=%async_computation | async-start | bytes 8388608 | tf_op jit(solution)/shard_map/all_to_all | solution.py:20
  24.2 0.0 copy-done.3
  24.2 0.2 copy.36
  24.4 0.0 copy-start.5
  24.4 2.4 broadcast_multiply_fusion.1
  26.8 7.8 %mul.77 = bf16[512,512]{1,0:T(8,128)(2,1)S(1)} reshape(bf16[32,16,32,16]{3,2,1,0:T(8,128)(2,1)} %broadcast_multiply_fusion.1) | data formatting | bytes 1048576 | tf_op jit(solution)/shard_map/mul | solution.py:36
  34.6 82.1 %all-to-all-done = bf16[4,128,8,512]{3,2,0,1:T(8,128)(2,1)} async-done(((bf16[4,128,8,512]{3,2,0,1:T(8,128)(2,1)}), bf16[4,128,8,512]{3,2,0,1:T(8,128)(2,1)}, u32[]{:S(2)}, u32[]{:S(2)}) %all-to-all-start) | async-done | bytes 4194336 | tf_op jit(solution)/shard_map/all_to_all | solution.py:20
  116.6 0.0 copy-done.5
  116.6 4.9 %convert_bitcast_fusion.1 = bf16[512,8,512]{2,0,1:T(8,128)(2,1)S(1)} fusion(bf16[512,8,512]{2,1,0:T(8,128)(2,1)} %bitcast.6, bf16[512,512]{1,0:T(8,128)(2,1)S(1)} %copy-done.5), kind=kOutput, calls=%fused_computation.19 | convolution fusion | flops 2149580800 | bytes 8912896 | tf_op jit(solution)/shard_map/im,iokc->mokc/dot_general | solution.py:8
  121.5 3.1 fusion.15
  124.6 102.8 %all_to_all.62 = bf16[512,1,8,512]{3,2,1,0:T(8,128)(2,1)S(1)} all-to-all(bf16[512,1,8,512]{3,2,1,0:T(8,128)(2,1)S(1)} %fusion.15), channel_id=1, replica_groups=mesh['seq'=128,'ch'=2] {'seq'}, dimensions={0} | all-to-all | bytes 8388608 | tf_op jit(solution)/shard_map/all_to_all | solution.py:24
  227.4 2.4 copy.38
  229.9 0.0 copy-start.2
  229.9 6.0 %all-to-all-start.2 = ((bf16[2,2048,512]{2,1,0:T(8,128)(2,1)}), bf16[2,2048,512]{2,1,0:T(8,128)(2,1)}, u32[]{:S(2)}, u32[]{:S(2)}) async-start(bf16[2,2048,512]{2,1,0:T(8,128)(2,1)} %bitcast.53), calls=%async_computation.2 | async-start | bytes 8388608 | tf_op jit(solution)/shard_map/all_to_all | solution.py:56
  235.8 0.0 copy-done.2
  235.8 0.2 copy.40
  236.0 11.0 %broadcast_multiply_fusion = bf16[64,16,64,16]{3,2,1,0:T(8,128)(2,1)} fusion(bf16[16,16]{1,0:T(8,128)(2,1)S(1)} %fusion.21, bf16[64,16,64]{2,1,0:T(8,128)(2,1)S(1)} %copy.40), kind=kLoop, calls=%fused_computation.11 | loop fusion | flops 1048576 | bytes 2228736 | tf_op jit(solution)/shard_map/mul | solution.py:53
  247.0 29.1 %mul.81 = bf16[1024,1024]{1,0:T(8,128)(2,1)S(1)} reshape(bf16[64,16,64,16]{3,2,1,0:T(8,128)(2,1)} %broadcast_multiply_fusion) | data formatting | bytes 4194304 | tf_op jit(solution)/shard_map/mul | solution.py:53
  276.1 102.0 %all-to-all-done.2 = bf16[2,2048,512]{2,1,0:T(8,128)(2,1)} async-done(((bf16[2,2048,512]{2,1,0:T(8,128)(2,1)}), bf16[2,2048,512]{2,1,0:T(8,128)(2,1)}, u32[]{:S(2)}, u32[]{:S(2)}) %all-to-all-start.2) | async-done | bytes 4194336 | tf_op jit(solution)/shard_map/all_to_all | solution.py:56
  378.1 6.2 %copy.39 = bf16[2048,2,512]{0,2,1:T(8,128)(2,1)} copy(bf16[2048,2,512]{2,0,1:T(8,128)(2,1)} %bitcast.15) | data formatting | bytes 8388608 | tf_op jit(solution)/shard_map/all_to_all | solution.py:56
  384.3 7.0 %convolution_convert_fusion.1 = bf16[2048,1024]{0,1:T(8,128)(2,1)S(1)} fusion(bf16[2048,1024]{0,1:T(8,128)(2,1)} %bitcast.56, bf16[1024,1024]{1,0:T(8,128)(2,1)S(1)} %mul.81), kind=kOutput, calls=%fused_computation.20 | convolution fusion | flops 4297064448 | bytes 10485760 | tf_op jit(solution)/shard_map/dot_general | solution.py:57
  391.3 54.5 %all_to_all.63 = bf16[2048,2,512]{0,2,1:T(8,128)(2,1)S(1)} all-to-all(bf16[2048,2,512]{0,2,1:T(8,128)(2,1)S(1)} %bitcast.57), channel_id=1, replica_groups=mesh['seq'=128,'ch'=2] {'ch'}, dimensions={1} | all-to-all | bytes 8388608 | tf_op jit(solution)/shard_map/all_to_all | solution.py:29
  445.8 4.3 convert_bitcast_fusion
  450.1 8.7 %copy.41 = f32[2,2048,512]{2,1,0:T(8,128)} copy(f32[2,2048,512]{1,2,0:T(8,128)} %convert_bitcast_fusion) | data formatting | bytes 16777216 | tf_op jit(solution)/shard_map/convert_element_type | solution.py:62
  458.8 0.0 copy-done.4
  458.8 7.6 %fusion.7 = bf16[4096,512]{1,0:T(8,128)(2,1)} fusion(f32[2,2048,512]{2,1,0:T(8,128)} %copy.41, bf16[4096,512]{1,0:T(8,128)(2,1)} %param.7, f32[512]{0:T(512)S(1)} %copy-done.4), kind=kLoop, calls=%fused_computation.12 | loop fusion | flops 18874368 | bytes 16779264 | tf_op jit(solution)/shard_map/convert_element_type | solution.py:63
  466.3 0.0 copy-done.1
  (4 shorter events, 0.0 us)
Async XLA Ops:
  0.0 1.6 copy-start
  11.2 13.0 %copy-start.3 = (bf16[32,16,16]{0,2,1:T(8,128)(2,1)S(1)}, bf16[32,16,16]{0,2,1:T(8,128)(2,1)}, u32[]{:S(2)}) copy-start(bf16[32,16,16]{0,2,1:T(8,128)(2,1)} %param.11) | copy-start | bytes 49156
  11.2 105.4 %all-to-all-start = ((bf16[4,128,8,512]{3,2,0,1:T(8,128)(2,1)}), bf16[4,128,8,512]{3,2,0,1:T(8,128)(2,1)}, u32[]{:S(2)}, u32[]{:S(2)}) async-start(bf16[4,128,8,512]{3,2,0,1:T(8,128)(2,1)} %copy.32), calls=%async_computation | async-start | bytes 8388608 | tf_op jit(solution)/shard_map/all_to_all | solution.py:20
  24.4 92.2 %copy-start.5 = (bf16[512,512]{1,0:T(8,128)(2,1)S(1)}, bf16[512,512]{1,0:T(8,128)(2,1)}, u32[]{:S(2)}) copy-start(bf16[512,512]{1,0:T(8,128)(2,1)} %param.10) | copy-start | bytes 1572868
  229.9 6.0 %copy-start.2 = (bf16[16,64,64]{2,1,0:T(8,128)(2,1)S(1)}, bf16[16,64,64]{2,1,0:T(8,128)(2,1)}, u32[]{:S(2)}) copy-start(bf16[16,64,64]{2,1,0:T(8,128)(2,1)} %param.12) | copy-start | bytes 393220
  229.9 148.3 %all-to-all-start.2 = ((bf16[2,2048,512]{2,1,0:T(8,128)(2,1)}), bf16[2,2048,512]{2,1,0:T(8,128)(2,1)}, u32[]{:S(2)}, u32[]{:S(2)}) async-start(bf16[2,2048,512]{2,1,0:T(8,128)(2,1)} %bitcast.53), calls=%async_computation.2 | async-start | bytes 8388608 | tf_op jit(solution)/shard_map/all_to_all | solution.py:56
  450.1 8.7 %copy-start.4 = (f32[512]{0:T(512)S(1)}, f32[512]{0:T(512)}, u32[]{:S(2)}) copy-start(f32[512]{0:T(512)} %param.13) | copy-start | bytes 6148
  458.8 7.6 %copy-start.1 = (bf16[1024,1024]{1,0:T(8,128)(2,1)S(1)}, bf16[1024,1024]{1,0:T(8,128)(2,1)}, u32[]{:S(2)}) copy-start(bf16[1024,1024]{1,0:T(8,128)(2,1)} %param.9) | copy-start | bytes 6291460
where the time goes:
time: 467 us; the launch traced here: 466 us
  waiting for transfers between devices  184 us (39%)
  blocking collectives  157 us (34%)
  local copies, waits for them, and re-layouts  58.7 us (13%)
  other arithmetic  25.2 us (5%)
  matrix products  22 us (5%)
  starting transfers between devices  18.9 us (4%)
    all_to_all x1, blocking collectives, restore_order(): lax.all_to_all(blocked, 'seq', split_axis=0, concat_axis=1, tiled=True)  103 us
    all_to_all x1, waiting for transfers between devices, per_device(): lax.all_to_all(blocked_all, 'ch', split_axis=0, concat_axis=1, tiled=True)  102 us
    all_to_all x1, waiting for transfers between devices, restore_order(): lax.all_to_all(segmented, 'seq', split_axis=1, concat_axis=0, tiled=True)  82.1 us
    all_to_all x1, blocking collectives, send_back(): lax.all_to_all(spread_half, 'ch', split_axis=1, concat_axis=0, tiled=True)  54.5 us
    mul x1, local copies, waits for them, and re-layouts, per_device(): spread_mix.transpose(1, 0, 2)[:, :, :, None] * inner_mask[None, :, None, :]  29.1 us
    all_to_all x1, starting transfers between devices, restore_order(): lax.all_to_all(segmented, 'seq', split_axis=1, concat_axis=0, tiled=True)  13 us
    mul x1, other arithmetic, per_device(): spread_mix.transpose(1, 0, 2)[:, :, :, None] * inner_mask[None, :, None, :]  11 us
  transfers between devices with their start and end apart: 2, of which 2 were waited for; matrix products, arithmetic and copies ran while one was open for 11% of the time, Pallas kernels for 0%

commit v1 on v0

v1 whole, which is shorter than its diff:
```python
import jax
import jax.numpy as jnp
from jax import lax
from jax.sharding import PartitionSpec as P

F32 = jnp.float32
BF16 = jnp.bfloat16


def channel_matrix(block_mix, spread_mix):
    groups, width, _ = block_mix.shape
    chans = groups * width
    col = lax.broadcasted_iota(jnp.int32, (width, chans), 1) % width
    tile = (col == lax.broadcasted_iota(jnp.int32, (width, chans), 0)).astype(BF16)
    row = lax.broadcasted_iota(jnp.int32, (chans, groups), 0) // width
    repeat = (row == lax.broadcasted_iota(jnp.int32, (chans, groups), 1)).astype(BF16)
    spread_rows = spread_mix.transpose(1, 2, 0).reshape(groups, chans)
    blocks = jnp.dot(block_mix.reshape(chans, width), tile, preferred_element_type=F32)
    spreads = jnp.dot(repeat, spread_rows, preferred_element_type=F32)
    return (blocks * spreads).astype(BF16)


def per_device(signal, twiddle, row_factor, col_factor, block_mix, spread_mix, gate_scale):
    seq_count = lax.axis_size("seq")
    ch_count = lax.axis_size("ch")
    count = seq_count * ch_count
    rows, cols = twiddle.shape
    width = signal.shape[1]
    each = cols // count
    lattice = signal.reshape(rows, cols, width)
    block_all = lax.all_gather(block_mix, "ch", axis=0, tiled=True)
    chan = channel_matrix(block_all, spread_mix)
    mixed = jnp.einsum("ijc,jk->kic", lattice, row_factor, preferred_element_type=F32)
    mixed = (mixed * twiddle.T[:, :, None]).astype(BF16).reshape(count, each * rows, width)
    arrived = lax.all_to_all(mixed, ("seq", "ch"), split_axis=0, concat_axis=0, tiled=True)
    arrived = arrived.reshape(seq_count, ch_count, each, rows, width)
    weights = col_factor.reshape(seq_count, rows, seq_count * rows)
    mixed_cols = jnp.einsum("slm,sgklc->mkgc", weights, arrived, preferred_element_type=F32).astype(BF16)
    spread = jnp.dot(mixed_cols.reshape(-1, ch_count * width), chan, preferred_element_type=F32).astype(BF16)
    spread = spread.reshape(seq_count, rows * each, ch_count, width).transpose(0, 2, 1, 3)
    spread = spread.reshape(count, rows * each, width)
    back = lax.all_to_all(spread, ("seq", "ch"), split_axis=0, concat_axis=0, tiled=True)
    back = back.reshape(count, rows, each, width).transpose(1, 0, 2, 3).reshape(signal.shape)
    signal32 = signal.astype(F32)
    gated = jax.nn.silu(gate_scale[None, :] * signal32) * back.astype(F32)
    return (signal32 + gated).astype(BF16)


def solution(mesh):
    placed = (P("seq", "ch"), P("seq", None), P(), P(), P("ch", None, None), P(), P("ch"))
    return jax.shard_map(
        per_device, mesh=mesh, in_specs=placed, out_specs=P("seq", "ch"), check_vma=False
    )
```

time: 467 us -> 337 us (0.72)
  waiting for transfers between devices: 184 us -> 0.01 us
  blocking collectives: 157 us -> 204 us
  local copies, waits for them, and re-layouts: 58.7 us -> 76.5 us
  other arithmetic: 25.2 us -> 7.59 us
  matrix products: 22 us -> 29 us
    all_to_all x2 -> x1, waiting for transfers between devices: 184 us -> 0.01 us  [per_device(): lax.all_to_all(mixed, ('seq', 'ch'), split_axis=0, concat_axis=0, tiled=T...]
    all_gather x0 -> x1, blocking collectives: none -> 98.8 us  [per_device(): block_all = lax.all_gather(block_mix, 'ch', axis=0, tiled=True)]
    all_to_all x2 -> x1, blocking collectives: 157 us -> 105 us  [per_device(): lax.all_to_all(spread, ('seq', 'ch'), split_axis=0, concat_axis=0, tiled=...]
    mul x2 -> x0, local copies, waits for them, and re-layouts: 36.8 us -> none  [the longest x1 29.1 us: per_device(): spread_mix.transpose(1, 0, 2)[:, :, :, None] * inner_mask[None, :, None, :]]
    convert_element_type x1 -> x5, local copies, waits for them, and re-layouts: 8.68 us -> 44.2 us  [the longest x3 27.7 us: per_device(): gated = jax.nn.silu(gate_scale[None, :] * signal32) * back.astype(F32)]
    reshape x1 -> x5, local copies, waits for them, and re-layouts: 2.62 us -> 25 us  [the longest x2 11.1 us: per_device(): spread.reshape(seq_count, rows * each, ch_count, width)]
    mul x2 -> x0, other arithmetic: 13.4 us -> none  [the longest x1 11 us: per_device(): spread_mix.transpose(1, 0, 2)[:, :, :, None] * inner_mask[None, :, None, :]]
    all_to_all x2 -> x0, local copies, waits for them, and re-layouts: 8.6 us -> none  [the longest x1 6.19 us: per_device(): lax.all_to_all(blocked_all, 'ch', split_axis=0, concat_axis=1, tiled=True)]
  transfers between devices with their start and end apart: 2 -> 1, of which waited for: 2 -> 0; matrix products, arithmetic and copies ran while one was open for 11% -> 1% of each run, Pallas kernels for 0% -> 0%
where the time goes in v1:
time: 337 us; the launch traced here: 332 us
  blocking collectives  204 us (61%)
  local copies, waits for them, and re-layouts  76.5 us (23%)
  matrix products  29 us (9%)
  starting transfers between devices  15.3 us (5%)
  other arithmetic  7.59 us (2%)
    all_to_all x1, blocking collectives, per_device(): lax.all_to_all(spread, ('seq', 'ch'), split_axis=0, concat_axis=0, tiled=...  105 us
    all_gather x1, blocking collectives, per_device(): block_all = lax.all_gather(block_mix, 'ch', axis=0, tiled=True)  98.8 us
    convert_element_type x3, local copies, waits for them, and re-layouts, per_device(): gated = jax.nn.silu(gate_scale[None, :] * signal32) * back.astype(F32)  27.7 us
    all_to_all x1, starting transfers between devices, per_device(): lax.all_to_all(mixed, ('seq', 'ch'), split_axis=0, concat_axis=0, tiled=T...  15.3 us
    convert_element_type x1, local copies, waits for them, and re-layouts, per_device(): jnp.einsum('slm,sgklc->mkgc', weights, arrived, preferred_element_type=F32)  11.3 us
    reshape x2, local copies, waits for them, and re-layouts, per_device(): spread.reshape(seq_count, rows * each, ch_count, width)  11.1 us
    dot_general x1, matrix products, per_device(): jnp.dot(mixed_cols.reshape(-1, ch_count * width), chan, preferred_element...  9.53 us
    dot_general x1, matrix products, per_device(): jnp.einsum('slm,sgklc->mkgc', weights, arrived, preferred_element_type=F32)  9.42 us
  transfers between devices with their start and end apart: 1, of which 0 were waited for; matrix products, arithmetic and copies ran while one was open for 1% of the time, Pallas kernels for 0%

profile of v1, /device:TPU:38, one launch (start us, length us, event | category | flops | bytes accessed | tf_op | source)
XLA Modules:
  0.0 332.4 jit_solution(15942502786852867862)
XLA Ops:
  0.0 0.0 copy-start
  0.0 1.6 copy-done
  1.6 7.0 %multiply_convert_fusion = bf16[1024,4,512]{2,0,1:T(8,128)(2,1)S(1)} fusion(f32[1024,4]{0,1:T(4,128)} %bitcast.44, bf16[4,1024,512]{2,1,0:T(8,128)(2,1)} %bitcast.38, bf16[1024,1024]{1,0:T(8,128)(2,1)S(1)} %copy-done), kind=kOutput, calls=%fused_computation.9 | convolution fusion | flops 4299161600 | bytes 10502144 | tf_op jit(solution)/shard_map/ijc,jk->kic/dot_general | solution.py:33
  8.6 5.2 %copy.31 = bf16[1024,4,512]{2,1,0:T(4,128)(2,1)} copy(bf16[1024,4,512]{2,0,1:T(8,128)(2,1)S(1)} %multiply_convert_fusion) | data formatting | bytes 8388608 | tf_op jit(solution)/shard_map/convert_element_type | solution.py:34
  13.9 6.9 %reshape.36 = bf16[256,16,512]{2,1,0:T(8,128)(2,1)} reshape(bf16[1024,4,512]{2,1,0:T(4,128)(2,1)} %copy.31) | data formatting | bytes 8388608 | tf_op jit(solution)/shard_map/reshape | solution.py:34
  20.8 0.0 copy-start.4
  20.8 0.0 copy-start.3
  20.8 0.0 copy-start.2
  20.8 15.3 %all-to-all-start = ((bf16[256,16,512]{2,1,0:T(8,128)(2,1)}), bf16[256,16,512]{2,1,0:T(8,128)(2,1)}, u32[]{:S(2)}, u32[]{:S(2)}) async-start(bf16[256,16,512]{2,1,0:T(8,128)(2,1)} %reshape.36), calls=%async_computation | async-start | bytes 8388608 | tf_op jit(solution)/shard_map/all_to_all | solution.py:35
  36.1 0.0 copy-done.4
  36.1 0.2 copy.35
  36.3 0.0 copy-done.3
  36.3 0.3 copy.37
  36.6 0.0 copy-done.2
  36.6 0.1 reshape.38
  36.7 98.8 %all_gather.3 = bf16[64,16,16]{2,1,0:T(8,128)(2,1)S(1)} all-gather(bf16[32,16,16]{2,1,0:T(8,128)(2,1)S(1)} %copy.35), channel_id=1, replica_groups=mesh['seq'=128,'ch'=2] {'ch'}, dimensions={0}, use_global_device_ids=true | all-gather | bytes 49152 | tf_op jit(solution)/shard_map/all_gather | solution.py:31
  135.5 3.0 fusion.15
  138.5 0.0 all-to-all-done
  138.5 6.9 %reshape.37 = bf16[128,2,4,4,512]{4,3,2,1,0:T(4,128)(2,1)} reshape(bf16[256,16,512]{2,1,0:T(8,128)(2,1)} %all-to-all-done) | data formatting | bytes 8388608 | tf_op jit(solution)/shard_map/reshape | solution.py:36
  145.4 9.4 %fusion.7 = bf16[512,4,2,512]{0,3,1,2:T(8,128)(2,1)} fusion(bf16[128,2,4,4,512]{4,3,2,1,0:T(4,128)(2,1)} %reshape.37, bf16[128,4,512,1,1]{2,1,0,4,3:T(4,128)(2,1)S(1)} %bitcast.41), kind=kOutput, calls=%fused_computation.11 | convolution fusion | flops 2149580800 | bytes 8912896 | tf_op jit(solution)/shard_map/slm,sgklc->mkgc/dot_general | solution.py:38
  154.9 11.3 %copy.34 = bf16[512,4,2,512]{3,2,1,0:T(2,128)(2,1)} copy(bf16[512,4,2,512]{0,3,1,2:T(8,128)(2,1)} %fusion.7) | data formatting | bytes 8388608 | tf_op jit(solution)/shard_map/convert_element_type | solution.py:38
  166.1 5.4 %copy.50 = bf16[256,8,2,512]{3,1,2,0:T(8,128)(2,1)} copy(bf16[256,8,2,512]{3,2,1,0:T(2,128)(2,1)} %bitcast.36) | data formatting | bytes 8388608
  171.5 9.5 %convolution_convert_fusion = bf16[2048,1024]{1,0:T(8,128)(2,1)} fusion(bf16[2048,1024]{1,0:T(8,128)(2,1)} %bitcast.39, f32[1024,1024]{0,1:T(8,128)} %fusion.15, bf16[1024,16]{1,0:T(8,128)(2,1)S(1)} %bitcast.42, s32[1024]{0:T(1024)S(1)} %get-tuple-element.7, s32[1024]{0:T(1024)S(1)} %get-tuple-element.8, pred[1024]{0:T(1024)(128)(4,1)S(1)} %fusion.30), kind=kOutput, calls=%fused_computation.16 | convolution fusion | flops 4332748800 | bytes 12624896 | tf_op jit(solution)/shard_map/dot_general | solution.py:39
  181.0 7.8 %reshape.42 = bf16[128,16,2,512]{3,2,1,0:T(2,128)(2,1)} reshape(bf16[2048,1024]{1,0:T(8,128)(2,1)} %convolution_convert_fusion) | data formatting | bytes 8388608 | tf_op jit(solution)/shard_map/reshape | solution.py:40
  188.8 3.3 copy.39
  192.1 105.1 %all_to_all.10 = bf16[256,16,512]{2,1,0:T(8,128)(2,1)S(1)} all-to-all(bf16[256,16,512]{2,1,0:T(8,128)(2,1)S(1)} %bitcast.37), channel_id=1, replica_groups=mesh['seq'=128,'ch'=2] {'seq','ch'}, dimensions={0} | all-to-all | bytes 8388608 | tf_op jit(solution)/shard_map/all_to_all | solution.py:42
  297.2 5.7 %copy.40 = f32[256,16,512]{2,0,1:T(8,128)} copy(bf16[256,16,512]{2,1,0:T(8,128)(2,1)S(1)} %all_to_all.10) | data formatting | bytes 12582912 | tf_op jit(solution)/shard_map/convert_element_type | solution.py:45
  302.8 12.0 %copy.41 = f32[4,256,4,512]{3,2,1,0:T(4,128)} copy(f32[4,256,4,512]{3,1,2,0:T(8,128)} %bitcast.35) | data formatting | bytes 16777216 | tf_op jit(solution)/shard_map/convert_element_type | solution.py:45
  314.8 10.0 %reshape.44 = f32[4096,512]{1,0:T(8,128)} reshape(f32[4,256,4,512]{3,2,1,0:T(4,128)} %copy.41) | data formatting | bytes 16777216 | tf_op jit(solution)/shard_map/convert_element_type | solution.py:45
  324.8 0.0 copy-done.5
  324.8 7.6 %fusion.6 = bf16[4096,512]{1,0:T(8,128)(2,1)} fusion(f32[4096,512]{1,0:T(8,128)} %reshape.44, bf16[4096,512]{1,0:T(8,128)(2,1)} %param.7, f32[512]{0:T(512)S(1)} %copy-done.5), kind=kLoop, calls=%fused_computation.10 | loop fusion | flops 18874368 | bytes 16779264 | tf_op jit(solution)/shard_map/convert_element_type | solution.py:46
  332.4 0.0 copy-done.1
  (6 shorter events, 0.0 us)
Async XLA Ops:
  0.0 1.6 copy-start
  20.8 15.4 %copy-start.4 = (bf16[32,16,16]{0,2,1:T(8,128)(2,1)S(1)}, bf16[32,16,16]{0,2,1:T(8,128)(2,1)}, u32[]{:S(2)}) copy-start(bf16[32,16,16]{0,2,1:T(8,128)(2,1)} %param.11) | copy-start | bytes 49156
  20.8 15.5 %copy-start.3 = (bf16[16,64,64]{2,1,0:T(8,128)(2,1)S(1)}, bf16[16,64,64]{2,1,0:T(8,128)(2,1)}, u32[]{:S(2)}) copy-start(bf16[16,64,64]{2,1,0:T(8,128)(2,1)} %param.12) | copy-start | bytes 393220
  20.8 15.8 %copy-start.2 = (bf16[512,512]{1,0:T(8,128)(2,1)S(1)}, bf16[512,512]{1,0:T(8,128)(2,1)}, u32[]{:S(2)}) copy-start(bf16[512,512]{1,0:T(8,128)(2,1)} %param.10) | copy-start | bytes 1572868
  20.8 117.8 %all-to-all-start = ((bf16[256,16,512]{2,1,0:T(8,128)(2,1)}), bf16[256,16,512]{2,1,0:T(8,128)(2,1)}, u32[]{:S(2)}, u32[]{:S(2)}) async-start(bf16[256,16,512]{2,1,0:T(8,128)(2,1)} %reshape.36), calls=%async_computation | async-start | bytes 8388608 | tf_op jit(solution)/shard_map/all_to_all | solution.py:35
  314.8 10.0 %copy-start.5 = (f32[512]{0:T(512)S(1)}, f32[512]{0:T(512)}, u32[]{:S(2)}) copy-start(f32[512]{0:T(512)} %param.13) | copy-start | bytes 6148
  324.8 7.6 %copy-start.1 = (bf16[1024,1024]{1,0:T(8,128)(2,1)S(1)}, bf16[1024,1024]{1,0:T(8,128)(2,1)}, u32[]{:S(2)}) copy-start(bf16[1024,1024]{1,0:T(8,128)(2,1)} %param.9) | copy-start | bytes 6291460

commit v2 on v1

--- a/solution.py
+++ b/solution.py
@@ -1,6 +1,8 @@
 import jax
 import jax.numpy as jnp
 from jax import lax
+from jax.experimental import pallas as pl
+from jax.experimental.pallas import tpu as pltpu
 from jax.sharding import PartitionSpec as P
 
 F32 = jnp.float32
@@ -20,6 +22,41 @@
     return (blocks * spreads).astype(BF16)
 
 
+def exchange_kernel(send, recv, own_sem, send_sem, recv_sem):
+    seq, ch = lax.axis_index("seq"), lax.axis_index("ch")
+    mine = seq * 2 + ch
+    own = pltpu.make_async_copy(send.at[mine], recv.at[mine], own_sem)
+    own.start()
+
+    def body(n, carry):
+        other = (mine + n + 1) % 256
+        pltpu.make_async_remote_copy(
+            src_ref=send.at[other],
+            dst_ref=recv.at[mine],
+            send_sem=send_sem,
+            recv_sem=recv_sem,
+            device_id=(other // 2, other % 2),
+            device_id_type=pl.DeviceIdType.MESH,
+        ).start()
+        return carry
+
+    lax.fori_loop(0, 255, body, 0)
+    own.wait()
+    pltpu.make_async_copy(send.at[0:255], send.at[0:255], send_sem).wait()
+    pltpu.make_async_copy(recv.at[0:255], recv.at[0:255], recv_sem).wait()
+
+
+def exchange(blocks):
+    return pl.pallas_call(
+        exchange_kernel,
+        out_shape=jax.ShapeDtypeStruct(blocks.shape, blocks.dtype),
+        in_specs=[pl.BlockSpec(memory_space=pl.ANY)],
+        out_specs=pl.BlockSpec(memory_space=pl.ANY),
+        scratch_shapes=[pltpu.SemaphoreType.DMA, pltpu.SemaphoreType.DMA, pltpu.SemaphoreType.DMA],
+        compiler_params=pltpu.CompilerParams(has_side_effects=True),
+    )(blocks)
+
+
 def per_device(signal, twiddle, row_factor, col_factor, block_mix, spread_mix, gate_scale):
     seq_count = lax.axis_size("seq")
     ch_count = lax.axis_size("ch")
@@ -32,14 +69,14 @@
     chan = channel_matrix(block_all, spread_mix)
     mixed = jnp.einsum("ijc,jk->kic", lattice, row_factor, preferred_element_type=F32)
     mixed = (mixed * twiddle.T[:, :, None]).astype(BF16).reshape(count, each * rows, width)
-    arrived = lax.all_to_all(mixed, ("seq", "ch"), split_axis=0, concat_axis=0, tiled=True)
+    arrived = exchange(mixed)
     arrived = arrived.reshape(seq_count, ch_count, each, rows, width)
     weights = col_factor.reshape(seq_count, rows, seq_count * rows)
     mixed_cols = jnp.einsum("slm,sgklc->mkgc", weights, arrived, preferred_element_type=F32).astype(BF16)
     spread = jnp.dot(mixed_cols.reshape(-1, ch_count * width), chan, preferred_element_type=F32).astype(BF16)
     spread = spread.reshape(seq_count, rows * each, ch_count, width).transpose(0, 2, 1, 3)
     spread = spread.reshape(count, rows * each, width)
-    back = lax.all_to_all(spread, ("seq", "ch"), split_axis=0, concat_axis=0, tiled=True)
+    back = exchange(spread)
     back = back.reshape(count, rows, each, width).transpose(1, 0, 2, 3).reshape(signal.shape)
     signal32 = signal.astype(F32)
     gated = jax.nn.silu(gate_scale[None, :] * signal32) * back.astype(F32)

time: 337 us -> 344 us (1.021)
  Pallas kernels: 0 us -> 213 us
  blocking collectives: 204 us -> 13.3 us
  starting transfers between devices: 15.3 us -> 0 us
    pallas_call x0 -> x2, Pallas kernels: none -> 213 us  [exchange(): pl.pallas_call(exchange_kernel, out_shape=jax.ShapeDtypeStruct(blocks.sha...]
    all_to_all x1 -> x0, blocking collectives: 105 us -> none  [per_device(): lax.all_to_all(spread, ('seq', 'ch'), split_axis=0, concat_axis=0, tiled=...]
    all_gather x1, blocking collectives: 98.8 us -> 13.3 us  [per_device(): block_all = lax.all_gather(block_mix, 'ch', axis=0, tiled=True)]
    all_to_all x1 -> x0, starting transfers between devices: 15.3 us -> none  [per_device(): lax.all_to_all(mixed, ('seq', 'ch'), split_axis=0, concat_axis=0, tiled=T...]
    unnamed x14 -> x12, local copies, waits for them, and re-layouts: 7.13 us -> 6.69 us
  transfers between devices with their start and end apart: 1 -> 0, of which waited for: 0 -> 0; matrix products, arithmetic and copies ran while one was open for 1% -> 0% of each run, Pallas kernels for 0% -> 0%
where the time goes in v2:
time: 344 us; the launch traced here: 340 us
  Pallas kernels  213 us (62%)
  local copies, waits for them, and re-layouts  79.1 us (23%)
  matrix products  26.9 us (8%)
  blocking collectives  13.3 us (4%)
  other arithmetic  7.59 us (2%)
    pallas_call x2, Pallas kernels, exchange(): pl.pallas_call(exchange_kernel, out_shape=jax.ShapeDtypeStruct(blocks.sha...  213 us
    convert_element_type x3, local copies, waits for them, and re-layouts, per_device(): gated = jax.nn.silu(gate_scale[None, :] * signal32) * back.astype(F32)  26.6 us
    all_gather x1, blocking collectives, per_device(): block_all = lax.all_gather(block_mix, 'ch', axis=0, tiled=True)  13.3 us
    reshape x2, local copies, waits for them, and re-layouts, per_device(): spread.reshape(seq_count, rows * each, ch_count, width)  13.1 us
    convert_element_type x1, local copies, waits for them, and re-layouts, per_device(): jnp.einsum('slm,sgklc->mkgc', weights, arrived, preferred_element_type=F32)  11.3 us
    dot_general x1, matrix products, per_device(): jnp.dot(mixed_cols.reshape(-1, ch_count * width), chan, preferred_element...  9.53 us
    dot_general x1, matrix products, per_device(): jnp.einsum('slm,sgklc->mkgc', weights, arrived, preferred_element_type=F32)  9.41 us
    convert_element_type x1, other arithmetic, per_device(): return (signal32 + gated).astype(BF16)  7.57 us

profile of v2, /device:TPU:38, one launch (start us, length us, event | category | flops | bytes accessed | tf_op | source)
XLA Modules:
  0.0 339.6 jit_solution(17620324691940664506)
XLA Ops:
  0.0 0.0 copy-start
  0.0 0.0 copy-start.4
  0.0 1.1 copy.28
  1.2 13.3 %all_gather.3 = bf16[64,16,16]{2,1,0:T(8,128)(2,1)S(1)} all-gather(bf16[32,16,16]{2,1,0:T(8,128)(2,1)S(1)} %copy.28), channel_id=1, replica_groups=mesh['seq'=128,'ch'=2] {'ch'}, dimensions={0}, use_global_device_ids=true | all-gather | bytes 49152 | tf_op jit(solution)/shard_map/all_gather | solution.py:68
  14.5 1.2 copy.30
  15.7 1.2 reshape.38
  16.9 0.0 copy-start.2
  16.9 3.0 fusion.15
  19.9 0.0 copy-done
  19.9 0.0 copy-done.4
  19.9 0.2 copy-done.2
  20.1 5.0 %multiply_convert_fusion = bf16[1024,4,512]{2,0,1:T(8,128)(2,1)S(1)} fusion(f32[1024,4]{0,1:T(4,128)S(1)} %bitcast.42, bf16[4,1024,512]{2,1,0:T(8,128)(2,1)S(1)} %bitcast.36, bf16[1024,1024]{1,0:T(8,128)(2,1)S(1)} %copy-done), kind=kOutput, calls=%fused_computation.9 | convolution fusion | flops 4299161600 | bytes 10502144 | tf_op jit(solution)/shard_map/ijc,jk->kic/dot_general | solution.py:70
  25.1 5.2 %copy.24 = bf16[1024,4,512]{2,1,0:T(4,128)(2,1)} copy(bf16[1024,4,512]{2,0,1:T(8,128)(2,1)S(1)} %multiply_convert_fusion) | data formatting | bytes 8388608 | tf_op jit(solution)/shard_map/convert_element_type | solution.py:71
  30.3 7.0 %reshape.36.send = bf16[256,16,512]{2,1,0:T(8,128)(2,1)} reshape(bf16[1024,4,512]{2,1,0:T(4,128)(2,1)} %copy.24) | data formatting | bytes 8388608 | tf_op jit(solution)/shard_map/reshape | solution.py:71
  37.3 108.1 %shard_map.73 = bf16[256,16,512]{2,1,0:T(8,128)(2,1)} custom-call(bf16[256,16,512]{2,1,0:T(8,128)(2,1)} %reshape.36.send), custom_call_target="tpu_custom_call" | custom-call | tf_op jit(solution)/shard_map/pallas_call | solution.py:50
  145.4 6.9 %reshape.37 = bf16[128,2,4,4,512]{4,3,2,1,0:T(4,128)(2,1)} reshape(bf16[256,16,512]{2,1,0:T(8,128)(2,1)} %shard_map.73) | data formatting | bytes 8388608 | tf_op jit(solution)/shard_map/reshape | solution.py:73
  152.3 9.4 %fusion.7 = bf16[512,4,2,512]{0,3,1,2:T(8,128)(2,1)} fusion(bf16[128,2,4,4,512]{4,3,2,1,0:T(4,128)(2,1)} %reshape.37, bf16[128,4,512,1,1]{2,1,0,4,3:T(4,128)(2,1)S(1)} %bitcast.39), kind=kOutput, calls=%fused_computation.11 | convolution fusion | flops 2149580800 | bytes 8912896 | tf_op jit(solution)/shard_map/slm,sgklc->mkgc/dot_general | solution.py:75
  161.7 11.3 %copy.27 = bf16[512,4,2,512]{3,2,1,0:T(2,128)(2,1)} copy(bf16[512,4,2,512]{0,3,1,2:T(8,128)(2,1)} %fusion.7) | data formatting | bytes 8388608 | tf_op jit(solution)/shard_map/convert_element_type | solution.py:75
  173.0 5.3 %copy.42 = bf16[256,8,2,512]{3,1,2,0:T(8,128)(2,1)} copy(bf16[256,8,2,512]{3,2,1,0:T(2,128)(2,1)} %bitcast.34) | data formatting | bytes 8388608
  178.3 9.5 %convolution_convert_fusion = bf16[2048,1024]{1,0:T(8,128)(2,1)} fusion(bf16[2048,1024]{1,0:T(8,128)(2,1)} %bitcast.37, f32[1024,1024]{0,1:T(8,128)} %fusion.15, bf16[1024,16]{1,0:T(8,128)(2,1)S(1)} %bitcast.40, s32[1024]{0:T(1024)S(1)} %get-tuple-element.7, s32[1024]{0:T(1024)S(1)} %get-tuple-element.8, pred[1024]{0:T(1024)(128)(4,1)S(1)} %fusion.30), kind=kOutput, calls=%fused_computation.16 | convolution fusion | flops 4332748800 | bytes 12624896 | tf_op jit(solution)/shard_map/dot_general | solution.py:76
  187.9 7.8 %reshape.42 = bf16[128,16,2,512]{3,2,1,0:T(2,128)(2,1)} reshape(bf16[2048,1024]{1,0:T(8,128)(2,1)} %convolution_convert_fusion) | data formatting | bytes 8388608 | tf_op jit(solution)/shard_map/reshape | solution.py:77
  195.7 5.3 %copy.32 = bf16[128,16,2,512]{3,1,2,0:T(8,128)(2,1)} copy(bf16[128,16,2,512]{3,2,1,0:T(2,128)(2,1)} %reshape.42) | data formatting | bytes 8388608 | tf_op jit(solution)/shard_map/reshape | solution.py:77
  201.0 104.4 %shard_map.74 = bf16[256,16,512]{2,1,0:T(8,128)(2,1)} custom-call(bf16[256,16,512]{2,1,0:T(8,128)(2,1)} %bitcast.35), custom_call_target="tpu_custom_call" | custom-call | tf_op jit(solution)/shard_map/pallas_call | solution.py:50
  305.4 8.3 %reshape.45 = f32[256,4,4,512]{3,2,1,0:T(4,128)} reshape(bf16[256,16,512]{2,1,0:T(8,128)(2,1)} %shard_map.74) | data formatting | bytes 12582912 | tf_op jit(solution)/shard_map/convert_element_type | solution.py:82
  313.7 8.2 %copy.33 = f32[4,256,4,512]{3,2,1,0:T(4,128)} copy(f32[4,256,4,512]{3,2,0,1:T(4,128)} %bitcast.33) | data formatting | bytes 16777216 | tf_op jit(solution)/shard_map/convert_element_type | solution.py:82
  322.0 0.0 copy-start.3
  322.0 10.0 %reshape.44 = f32[4096,512]{1,0:T(8,128)} reshape(f32[4,256,4,512]{3,2,1,0:T(4,128)} %copy.33) | data formatting | bytes 16777216 | tf_op jit(solution)/shard_map/convert_element_type | solution.py:82
  332.0 0.0 copy-done.3
  332.0 0.0 copy-start.1
  332.0 7.6 %fusion.6 = bf16[4096,512]{1,0:T(8,128)(2,1)} fusion(f32[4096,512]{1,0:T(8,128)} %reshape.44, bf16[4096,512]{1,0:T(8,128)(2,1)} %param.7, f32[512]{0:T(512)S(1)} %copy-done.3), kind=kLoop, calls=%fused_computation.10 | loop fusion | flops 18874368 | bytes 16779264 | tf_op jit(solution)/shard_map/convert_element_type | solution.py:83
  339.6 0.0 copy-done.1
  (4 shorter events, 0.0 us)
Async XLA Ops:
  0.0 19.9 %copy-start = (bf16[1024,1024]{1,0:T(8,128)(2,1)S(1)}, bf16[1024,1024]{1,0:T(8,128)(2,1)}, u32[]{:S(2)}) copy-start(bf16[1024,1024]{1,0:T(8,128)(2,1)} %param.9) | copy-start | bytes 6291460
  0.0 19.9 %copy-start.4 = (f32[4,1024]{1,0:T(4,128)S(1)}, f32[4,1024]{1,0:T(4,128)}, u32[]{:S(2)}) copy-start(f32[4,1024]{1,0:T(4,128)} %param.8) | copy-start | bytes 49156
  16.9 3.2 copy-start.2
  322.0 10.0 %copy-start.3 = (f32[512]{0:T(512)S(1)}, f32[512]{0:T(512)}, u32[]{:S(2)}) copy-start(f32[512]{0:T(512)} %param.13) | copy-start | bytes 6148
  332.0 7.6 %copy-start.1 = (bf16[1024,1024]{1,0:T(8,128)(2,1)S(1)}, bf16[1024,1024]{1,0:T(8,128)(2,1)}, u32[]{:S(2)}) copy-start(bf16[1024,1024]{1,0:T(8,128)(2,1)} %param.9) | copy-start | bytes 6291460

commit v3 on v1

v3 whole, which is shorter than its diff:
```python
import jax
import jax.numpy as jnp
from jax import lax
from jax.experimental import pallas as pl
from jax.experimental.pallas import tpu as pltpu
from jax.sharding import PartitionSpec as P

F32 = jnp.float32
BF16 = jnp.bfloat16
NT = (((1,), (1,)), ((), ()))
TN = (((0,), (0,)), ((), ()))


def iota(shape, dim):
    return lax.broadcasted_iota(jnp.int32, shape, dim)


def dot(a, b):
    return jnp.dot(a, b, preferred_element_type=F32)


def rows_at(ref, start, size):
    return ref.at[pl.ds(pl.multiple_of(start, 16), size)]


def pair_of(x, y):
    return (x % 2) * 4 + (y + 2 * (x // 2)) % 4


def z_offset(n):
    odd = n % 2
    step = odd * ((n + 1) // 2) + (1 - odd) * (8 - n // 2)
    return (step - 4 * jnp.where(n == 0, 1, 0) + jnp.where(n == 7, 4, 0)) % 8


def kernel(
    signal_hbm, rowf_hbm, colf_hbm, tw_ref, block_ref, mix_ref, gate_ref,
    out_hbm,
    signal, rowf, colf, send1, recv1, expand, chan, send2, recv2, out, gates,
    weave, unweave, blocks, spread_rows,
    load_sem, own_sem, send_sem, recv1_sem, recv2_sem, block_sem, out_sem,
):
    seq, ch = lax.axis_index("seq"), lax.axis_index("ch")
    y, x, core = seq // 32, (seq // 2) % 4, seq % 2
    z = ch * 4 + (seq // 8) % 4
    mine = pair_of(x, y) * 32 + (x // 2) * 16 + z * 2 + core

    loads = [pltpu.make_async_copy(rowf_hbm, rowf, load_sem.at[0])]
    for i in range(4):
        part = pl.ds(i * 1024, 1024)
        loads.append(pltpu.make_async_copy(signal_hbm.at[part], signal.at[part], load_sem.at[1 + i]))
    loads.append(pltpu.make_async_copy(colf_hbm, colf, load_sem.at[5]))
    for load in loads:
        load.start()

    o, s = iota((512, 512), 0), iota((512, 512), 1)
    weave[...] = (s == ((o >> 2) & 3) * 128 + (o >> 4) * 4 + (o & 3)).astype(F32).astype(BF16)
    unweave[...] = (o == ((s >> 2) & 3) * 128 + (s >> 4) * 4 + (s & 3)).astype(F32).astype(BF16)
    eye = iota((128, 128), 0) == iota((128, 128), 1)
    eye16 = eye.astype(F32).astype(BF16)

    eye_small = (iota((16, 16), 0) == iota((16, 16), 1)).astype(F32).astype(BF16)
    flipped = lax.dot_general(eye_small, block_ref[...], NT, preferred_element_type=F32)
    blocks[pl.ds(pl.multiple_of(ch * 16, 16), 16), :] = flipped.astype(BF16)
    block_copy = pltpu.make_async_remote_copy(
        src_ref=rows_at(blocks, ch * 16, 16), dst_ref=rows_at(blocks, ch * 16, 16),
        send_sem=block_sem.at[0], recv_sem=block_sem.at[1],
        device_id=(seq, 1 - ch), device_id_type=pl.DeviceIdType.MESH,
    )
    block_copy.start()
    for load in loads:
        load.wait()

    def send_tile(pair, source, target, recv_sem, source_row, own):
        def body(n, carry):
            half, far_core = n // 16, (n // 8) % 2
            far_z = (z + z_offset(n % 8)) % 8
            far_x, far_y = pair // 4 + 2 * half, (pair % 4 + 2 * half) % 4
            far_seq = far_y * 32 + (far_z % 4) * 8 + far_x * 2 + far_core
            far_ch = far_z // 4
            src = rows_at(source, source_row(half, far_z, far_core) * 16, 16)
            is_self = jnp.logical_and(far_seq == seq, far_ch == ch)

            @pl.when(is_self)
            def _():
                pltpu.make_async_copy(src, rows_at(target[0], target[1] * 16, 16), own).start()

            @pl.when(jnp.logical_not(is_self))
            def _():
                pltpu.make_async_remote_copy(
                    src_ref=src, dst_ref=rows_at(target[0], target[1] * 16, 16),
                    send_sem=send_sem, recv_sem=recv_sem,
                    device_id=(far_seq, far_ch), device_id_type=pl.DeviceIdType.MESH,
                ).start()

            return carry

        lax.fori_loop(0, 32, body, 0)

    def row_step(t, carry):
        pair = pair_of((x + t // 4) % 4, (y + t % 4) % 4)
        lanes = pl.ds(pl.multiple_of(pair * 128, 128), 128)
        weights = lax.dot_general(eye16, rowf[:, lanes], NT, preferred_element_type=F32).astype(BF16)
        parts = []
        for i in range(4):
            mixed = dot(weights, signal[i * 1024:(i + 1) * 1024, :])
            scale = jnp.sum(jnp.where(eye, tw_ref[i:i + 1, lanes], 0.0), axis=1, keepdims=True)
            parts.append((mixed * scale).astype(BF16))
        woven = dot(weave[...], jnp.concatenate(parts, axis=0)).astype(BF16)
        send1[pl.ds(pl.multiple_of(pair * 512, 512), 512), :] = woven
        send_tile(
            pair, send1, (recv1, ch * 128 + seq), recv1_sem,
            lambda half, far_z, far_core: pair * 32 + half * 16 + far_z * 2 + far_core, own_sem.at[0],
        )
        return carry

    lax.fori_loop(0, 8, row_step, 0)

    def gate_step(n, carry):
        part = pl.ds(pl.multiple_of(n * 64, 64), 64)
        v = gate_ref[...] * signal[part, :].astype(F32)
        gates[part, :] = v / (1.0 + jnp.exp(-v))
        return carry

    lax.fori_loop(0, 64, gate_step, 0)

    def expand_step(pair, carry):
        r = iota((256, 512), 0)
        half = r >> 7
        far_seq = ((pair % 4 + 2 * half) & 3) * 32 + ((r >> 5) & 3) * 8 + (pair // 4 + 2 * half) * 2 + ((r >> 4) & 1)
        pick = (iota((256, 512), 1) == far_seq * 4 + ((r >> 2) & 3)).astype(F32).astype(BF16)
        taken = lax.dot_general(pick, colf[...], NT, preferred_element_type=F32).astype(BF16)
        widen = (iota((128, 512), 0) == (iota((128, 512), 1) >> 2)).astype(F32).astype(BF16)
        same = (iota((256, 512), 0) & 3) == (iota((256, 512), 1) & 3)
        rows = pl.ds(pl.multiple_of(pair * 256, 256), 256)
        for j in range(4):
            wide = dot(taken[:, j * 128:(j + 1) * 128], widen)
            expand[rows, j * 512:(j + 1) * 512] = jnp.where(same, wide, 0.0).astype(BF16)
        return carry

    lax.fori_loop(0, 8, expand_step, 0)

    spread_rows[...] = jnp.zeros_like(spread_rows)

    def spread_step(r, carry):
        place = (iota((64, 1024), 1) == iota((64, 1024), 0) * 16 + r).astype(F32).astype(BF16)
        spread_rows[...] += dot(mix_ref[pl.ds(pl.multiple_of(r * 64, 64), 64), :], place)
        return carry

    lax.fori_loop(0, 16, spread_step, 0)
    block_copy.wait()
    tile = ((iota((16, 1024), 1) & 15) == iota((16, 1024), 0)).astype(F32).astype(BF16)
    repeat = ((iota((256, 16), 0) >> 4) == iota((256, 16), 1)).astype(F32).astype(BF16)
    for g in range(2):
        for q in range(2):
            left = lax.dot_general(
                blocks[g * 16:(g + 1) * 16, q * 256:(q + 1) * 256], tile, TN, preferred_element_type=F32
            )
            p0 = g * 32 + q * 16
            right = dot(repeat, spread_rows[p0:p0 + 16, :].astype(BF16))
            chan[p0 * 16:p0 * 16 + 256, :] = (left * right).astype(BF16)

    pltpu.make_async_copy(rows_at(recv1, 0, 16), rows_at(recv1, 0, 16), own_sem.at[0]).wait()
    pltpu.make_async_copy(rows_at(recv1, 0, 255 * 16), rows_at(recv1, 0, 255 * 16), recv1_sem).wait()

    def col_step(t, carry):
        pair = pair_of((x + t // 4) % 4, (y + t % 4) % 4)
        weights = expand[pl.ds(pl.multiple_of(pair * 256, 256), 256), :]
        low = dot(weights, recv1[0:2048, :]).astype(BF16)
        high = dot(weights, recv1[2048:4096, :]).astype(BF16)
        for h in range(2):
            cut = slice(h * 512, (h + 1) * 512)
            mixed = dot(low, chan[0:512, cut]) + dot(high, chan[512:1024, cut])
            send2[pl.ds(pl.multiple_of((pair * 2 + h) * 256, 256), 256), :] = mixed.astype(BF16)
        send_tile(
            pair, send2, (recv2, mine), recv2_sem.at[t],
            lambda half, far_z, far_core: (pair * 2 + far_z // 4) * 16 + half * 8 + (far_z % 4) * 2 + far_core,
            own_sem.at[1],
        )
        return carry

    lax.fori_loop(0, 8, col_step, 0)
    pltpu.make_async_copy(rows_at(recv2, 0, 16), rows_at(recv2, 0, 16), own_sem.at[1]).wait()

    def last_step(t, own):
        pair = pair_of((x - t // 4 + 4) % 4, (y - t % 4 + 4) % 4)
        got = rows_at(recv2, pair * 512, 512 - own)
        pltpu.make_async_copy(got, got, recv2_sem.at[t]).wait()
        spread = dot(unweave[...], recv2[pl.ds(pl.multiple_of(pair * 512, 512), 512), :])
        for i in range(4):
            part = pl.ds(pl.multiple_of(i * 1024 + pair * 128, 128), 128)
            out[part, :] = (signal[part, :].astype(F32) + gates[part, :] * spread[i * 128:(i + 1) * 128, :]).astype(BF16)
            pltpu.make_async_copy(out.at[part], out_hbm.at[part], out_sem).start()

    last_step(0, 16)

    def rest(t, carry):
        last_step(t, 0)
        return carry

    lax.fori_loop(1, 8, rest, 0)
    pltpu.make_async_copy(out, out_hbm, out_sem).wait()
    pltpu.make_async_copy(rows_at(send1, 0, 255 * 16), rows_at(send1, 0, 255 * 16), send_sem).wait()
    pltpu.make_async_copy(rows_at(send2, 0, 255 * 16), rows_at(send2, 0, 255 * 16), send_sem).wait()


def per_device(signal, twiddle, row_factor, col_factor, block_mix, spread_mix, gate_scale):
    groups, width, _ = block_mix.shape
    anywhere = pl.BlockSpec(memory_space=pl.ANY)
    inside = pl.BlockSpec(memory_space=pltpu.VMEM)
    dma = pltpu.SemaphoreType.DMA
    return pl.pallas_call(
        kernel,
        out_shape=jax.ShapeDtypeStruct(signal.shape, signal.dtype),
        in_specs=[anywhere, anywhere, anywhere, inside, inside, inside, inside],
        out_specs=anywhere,
        scratch_shapes=[
            pltpu.VMEM((4096, 512), BF16),
            pltpu.VMEM((1024, 1024), BF16),
            pltpu.VMEM((512, 512), BF16),
            pltpu.VMEM((4096, 512), BF16),
            pltpu.VMEM((4096, 512), BF16),
            pltpu.VMEM((2048, 2048), BF16),
            pltpu.VMEM((1024, 1024), BF16),
            pltpu.VMEM((4096, 512), BF16),
            pltpu.VMEM((4096, 512), BF16),
            pltpu.VMEM((4096, 512), BF16),
            pltpu.VMEM((4096, 512), F32),
            pltpu.VMEM((512, 512), BF16),
            pltpu.VMEM((512, 512), BF16),
            pltpu.VMEM((32, 512), BF16),
            pltpu.VMEM((64, 1024), F32),
            dma((6,)), dma((2,)), dma, dma, dma((8,)), dma((2,)), dma,
        ],
        compiler_params=pltpu.CompilerParams(has_side_effects=True, vmem_limit_bytes=58 << 20),
    )(
        signal, row_factor, col_factor, twiddle, block_mix.reshape(groups * width, width),
        spread_mix.reshape(-1, spread_mix.shape[2]), gate_scale.reshape(1, -1),
    )


def solution(mesh):
    placed = (P("seq", "ch"), P("seq", None), P(), P(), P("ch", None, None), P(), P("ch"))
    return jax.shard_map(
        per_device, mesh=mesh, in_specs=placed, out_specs=P("seq", "ch"), check_vma=False
    )
```

time: 337 us -> 218 us (0.65)
  Pallas kernels: 0 us -> 209 us
  blocking collectives: 204 us -> 0 us
  local copies, waits for them, and re-layouts: 76.5 us -> 6.12 us
  matrix products: 29 us -> 0 us
  starting transfers between devices: 15.3 us -> 0 us
  other arithmetic: 7.59 us -> 0 us
    pallas_call x0 -> x1, Pallas kernels: none -> 209 us  [per_device(): pl.pallas_call(kernel, out_shape=jax.ShapeDtypeStruct(signal.shape, signa...]
    all_to_all x1 -> x0, blocking collectives: 105 us -> none  [per_device(): lax.all_to_all(spread, ('seq', 'ch'), split_axis=0, concat_axis=0, tiled=...]
    all_gather x1 -> x0, blocking collectives: 98.8 us -> none  [per_device(): block_all = lax.all_gather(block_mix, 'ch', axis=0, tiled=True)]
    convert_element_type x5 -> x0, local copies, waits for them, and re-layouts: 44.2 us -> none  [the longest x3 27.7 us: per_device(): gated = jax.nn.silu(gate_scale[None, :] * signal32) * back.astype(F32)]
    dot_general x4 -> x0, matrix products: 29 us -> none  [the longest x1 9.53 us: per_device(): jnp.dot(mixed_cols.reshape(-1, ch_count * width), chan, preferred_element...]
    reshape x5 -> x0, local copies, waits for them, and re-layouts: 25 us -> none  [the longest x2 11.1 us: per_device(): spread.reshape(seq_count, rows * each, ch_count, width)]
    all_to_all x1 -> x0, starting transfers between devices: 15.3 us -> none  [per_device(): lax.all_to_all(mixed, ('seq', 'ch'), split_axis=0, concat_axis=0, tiled=T...]
    convert_element_type x1 -> x0, other arithmetic: 7.57 us -> none  [per_device(): return (signal32 + gated).astype(BF16)]
  transfers between devices with their start and end apart: 1 -> 0, of which waited for: 0 -> 0; matrix products, arithmetic and copies ran while one was open for 1% -> 0% of each run, Pallas kernels for 0% -> 0%
where the time goes in v3:
time: 218 us; the launch traced here: 215 us
  Pallas kernels  209 us (96%)
  local copies, waits for them, and re-layouts  6.12 us (3%)
    pallas_call x1, Pallas kernels, per_device(): pl.pallas_call(kernel, out_shape=jax.ShapeDtypeStruct(signal.shape, signa...  209 us
    unnamed x2, local copies, waits for them, and re-layouts  6.12 us

profile of v3, /device:TPU:38, one launch (start us, length us, event | category | flops | bytes accessed | tf_op | source)
XLA Modules:
  0.0 214.8 jit_solution(10597508816338013345)
XLA Ops:
  0.0 1.6 copy.8
  1.6 208.7 %shard_map.73 = bf16[4096,512]{1,0:T(8,128)(2,1)} custom-call(bf16[4096,512]{1,0:T(8,128)(2,1)} %signal_hbm.1, bf16[1024,1024]{1,0:T(8,128)(2,1)} %rowf_hbm.1, bf16[512,512]{1,0:T(8,128)(2,1)} %colf_hbm.1, f32[4,1024]{1,0:T(4,128)} %tw_ref.1, bf16[512,16]{1,0:T(8,128)(2,1)} %bitcast.3, bf16[1024,64]{1,0:T(8,128)(2,1)} %bitcast.4, f32[1,512]{1,0:T(1,128)} %bitcast.5), custom_call_target="tpu_custom_call" | custom-call | tf_op jit(solution)/shard_map/pallas_call | solution.py:212
  210.4 4.5 %copy.10 = bf16[4096,512]{1,0:T(8,128)(2,1)} copy(bf16[4096,512]{1,0:T(8,128)(2,1)} %shard_map.73) | data formatting | bytes 8388608

commit v4 on v3

--- a/solution.py
+++ b/solution.py
@@ -35,41 +35,64 @@
 
 def kernel(
     signal_hbm, rowf_hbm, colf_hbm, tw_ref, block_ref, mix_ref, gate_ref,
-    out_hbm,
-    signal, rowf, colf, send1, recv1, expand, chan, send2, recv2, out, gates,
+    out,
+    signal, rowf, colf, send1, recv1, expand, chan, send2, recv2, gates,
     weave, unweave, blocks, spread_rows,
-    load_sem, own_sem, send_sem, recv1_sem, recv2_sem, block_sem, out_sem,
+    load_sem, own_sem, send_sem, recv1_sem, recv2_sem, block_sem, plane_sem,
 ):
     seq, ch = lax.axis_index("seq"), lax.axis_index("ch")
     y, x, core = seq // 32, (seq // 2) % 4, seq % 2
     z = ch * 4 + (seq // 8) % 4
     mine = pair_of(x, y) * 32 + (x // 2) * 16 + z * 2 + core
 
-    loads = [pltpu.make_async_copy(rowf_hbm, rowf, load_sem.at[0])]
+    barrier = pltpu.get_barrier_semaphore()
+
+    def greet(sem, dx, dy, dz, dc):
+        far_z = (z + dz) % 8
+        far_seq = (y + dy) % 4 * 32 + far_z % 4 * 8 + (x + dx) % 4 * 2 + (core + dc) % 2
+        pl.semaphore_signal(
+            sem, inc=1, device_id=(far_seq, far_z // 4), device_id_type=pl.DeviceIdType.MESH
+        )
+
+    def greet_plane(sem):
+        def body(n, carry):
+            greet(sem, (n + 1) % 4, (n + 1) // 4, 0, 0)
+            return carry
+
+        lax.fori_loop(0, 15, body, 0)
+
+    def greet_line(n, carry):
+        greet(barrier, 0, 0, (n + 1) // 2, (n + 1) % 2)
+        return carry
+
+    loads = []
     for i in range(4):
         part = pl.ds(i * 1024, 1024)
         loads.append(pltpu.make_async_copy(signal_hbm.at[part], signal.at[part], load_sem.at[1 + i]))
+    loads = [pltpu.make_async_copy(rowf_hbm, rowf, load_sem.at[0])] + loads
     loads.append(pltpu.make_async_copy(colf_hbm, colf, load_sem.at[5]))
+    lax.fori_loop(0, 15, greet_line, 0)
+    greet_plane(barrier)
     for load in loads:
         load.start()
 
     o, s = iota((512, 512), 0), iota((512, 512), 1)
     weave[...] = (s == ((o >> 2) & 3) * 128 + (o >> 4) * 4 + (o & 3)).astype(F32).astype(BF16)
-    unweave[...] = (o == ((s >> 2) & 3) * 128 + (s >> 4) * 4 + (s & 3)).astype(F32).astype(BF16)
     eye = iota((128, 128), 0) == iota((128, 128), 1)
     eye16 = eye.astype(F32).astype(BF16)
 
-    eye_small = (iota((16, 16), 0) == iota((16, 16), 1)).astype(F32).astype(BF16)
-    flipped = lax.dot_general(eye_small, block_ref[...], NT, preferred_element_type=F32)
+    flipped = jnp.zeros((16, 512), F32)
+    for q in range(16):
+        place = (iota((32, 512), 1) == iota((32, 512), 0) * 16 + q).astype(F32).astype(BF16)
+        flipped += dot(block_ref[q * 16:(q + 1) * 16, :], place)
     blocks[pl.ds(pl.multiple_of(ch * 16, 16), 16), :] = flipped.astype(BF16)
     block_copy = pltpu.make_async_remote_copy(
         src_ref=rows_at(blocks, ch * 16, 16), dst_ref=rows_at(blocks, ch * 16, 16),
         send_sem=block_sem.at[0], recv_sem=block_sem.at[1],
         device_id=(seq, 1 - ch), device_id_type=pl.DeviceIdType.MESH,
     )
-    block_copy.start()
-    for load in loads:
-        load.wait()
+    pl.semaphore_wait(barrier, 30)
+    greet_plane(plane_sem)
 
     def send_tile(pair, source, target, recv_sem, source_row, own):
         def body(n, carry):
@@ -100,14 +123,29 @@
     def row_step(t, carry):
         pair = pair_of((x + t // 4) % 4, (y + t % 4) % 4)
         lanes = pl.ds(pl.multiple_of(pair * 128, 128), 128)
+
+        @pl.when(t == 0)
+        def _():
+            loads[0].wait()
+
         weights = lax.dot_general(eye16, rowf[:, lanes], NT, preferred_element_type=F32).astype(BF16)
         parts = []
         for i in range(4):
+            @pl.when(t == 0)
+            def _():
+                loads[1 + i].wait()
+
             mixed = dot(weights, signal[i * 1024:(i + 1) * 1024, :])
             scale = jnp.sum(jnp.where(eye, tw_ref[i:i + 1, lanes], 0.0), axis=1, keepdims=True)
             parts.append((mixed * scale).astype(BF16))
         woven = dot(weave[...], jnp.concatenate(parts, axis=0)).astype(BF16)
         send1[pl.ds(pl.multiple_of(pair * 512, 512), 512), :] = woven
+
+        @pl.when(t == 0)
+        def _():
+            pl.semaphore_wait(plane_sem, 15)
+            block_copy.start()
+
         send_tile(
             pair, send1, (recv1, ch * 128 + seq), recv1_sem,
             lambda half, far_z, far_core: pair * 32 + half * 16 + far_z * 2 + far_core, own_sem.at[0],
@@ -115,6 +153,8 @@
         return carry
 
     lax.fori_loop(0, 8, row_step, 0)
+
+    loads[5].wait()
 
     def gate_step(n, carry):
         part = pl.ds(pl.multiple_of(n * 64, 64), 64)
@@ -140,6 +180,7 @@
 
     lax.fori_loop(0, 8, expand_step, 0)
 
+    unweave[...] = (o == ((s >> 2) & 3) * 128 + (s >> 4) * 4 + (s & 3)).astype(F32).astype(BF16)
     spread_rows[...] = jnp.zeros_like(spread_rows)
 
     def spread_step(r, carry):
@@ -190,7 +231,6 @@
         for i in range(4):
             part = pl.ds(pl.multiple_of(i * 1024 + pair * 128, 128), 128)
             out[part, :] = (signal[part, :].astype(F32) + gates[part, :] * spread[i * 128:(i + 1) * 128, :]).astype(BF16)
-            pltpu.make_async_copy(out.at[part], out_hbm.at[part], out_sem).start()
 
     last_step(0, 16)
 
@@ -199,7 +239,6 @@
         return carry
 
     lax.fori_loop(1, 8, rest, 0)
-    pltpu.make_async_copy(out, out_hbm, out_sem).wait()
     pltpu.make_async_copy(rows_at(send1, 0, 255 * 16), rows_at(send1, 0, 255 * 16), send_sem).wait()
     pltpu.make_async_copy(rows_at(send2, 0, 255 * 16), rows_at(send2, 0, 255 * 16), send_sem).wait()
 
@@ -211,9 +250,9 @@
     dma = pltpu.SemaphoreType.DMA
     return pl.pallas_call(
         kernel,
-        out_shape=jax.ShapeDtypeStruct(signal.shape, signal.dtype),
+        out_shape=pltpu.VMEM(signal.shape, signal.dtype),
         in_specs=[anywhere, anywhere, anywhere, inside, inside, inside, inside],
-        out_specs=anywhere,
+        out_specs=inside,
         scratch_shapes=[
             pltpu.VMEM((4096, 512), BF16),
             pltpu.VMEM((1024, 1024), BF16),
@@ -222,7 +261,6 @@
             pltpu.VMEM((4096, 512), BF16),
             pltpu.VMEM((2048, 2048), BF16),
             pltpu.VMEM((1024, 1024), BF16),
-            pltpu.VMEM((4096, 512), BF16),
             pltpu.VMEM((4096, 512), BF16),
             pltpu.VMEM((4096, 512), BF16),
             pltpu.VMEM((4096, 512), F32),
@@ -230,11 +268,12 @@
             pltpu.VMEM((512, 512), BF16),
             pltpu.VMEM((32, 512), BF16),
             pltpu.VMEM((64, 1024), F32),
-            dma((6,)), dma((2,)), dma, dma, dma((8,)), dma((2,)), dma,
+            dma((6,)), dma((2,)), dma, dma, dma((8,)), dma((2,)), pltpu.SemaphoreType.REGULAR,
         ],
-        compiler_params=pltpu.CompilerParams(has_side_effects=True, vmem_limit_bytes=58 << 20),
+        compiler_params=pltpu.CompilerParams(
+            collective_id=0, has_side_effects=True, vmem_limit_bytes=52 << 20),
     )(
-        signal, row_factor, col_factor, twiddle, block_mix.reshape(groups * width, width),
+        signal, row_factor, col_factor, twiddle, block_mix.transpose(1, 2, 0).reshape(width * width, groups),
         spread_mix.reshape(-1, spread_mix.shape[2]), gate_scale.reshape(1, -1),
     )
 

time: 218 us -> 205 us (0.940)
  Pallas kernels: 209 us -> 200 us
  local copies, waits for them, and re-layouts: 6.12 us -> 2.02 us
    pallas_call x1, Pallas kernels: 209 us -> 200 us  [per_device(): pl.pallas_call(kernel, out_shape=pltpu.VMEM(signal.shape, signal.dtype),...]
    unnamed x2 -> x1, local copies, waits for them, and re-layouts: 6.12 us -> 2.02 us
where the time goes in v4:
time: 205 us; the launch traced here: 202 us
  Pallas kernels  200 us (98%)
    pallas_call x1, Pallas kernels, per_device(): pl.pallas_call(kernel, out_shape=pltpu.VMEM(signal.shape, signal.dtype),...  200 us

profile of v4, /device:TPU:38, one launch (start us, length us, event | category | flops | bytes accessed | tf_op | source)
XLA Modules:
  0.0 201.6 jit_solution(11756978973849622166)
XLA Ops:
  0.0 199.6 %shard_map.73 = bf16[4096,512]{1,0:T(8,128)(2,1)S(1)} custom-call(bf16[4096,512]{1,0:T(8,128)(2,1)} %signal_hbm.1, bf16[1024,1024]{1,0:T(8,128)(2,1)} %rowf_hbm.1, bf16[512,512]{1,0:T(8,128)(2,1)} %colf_hbm.1, f32[4,1024]{1,0:T(4,128)} %tw_ref.1, bf16[256,32]{1,0:T(8,128)(2,1)} %bitcast.6, bf16[1024,64]{1,0:T(8,128)(2,1)} %bitcast.5, f32[1,512]{1,0:T(1,128)} %bitcast.7), custom_call_target="tpu_custom_call" | custom-call | tf_op jit(solution)/shard_map/pallas_call | solution.py:251
  199.6 2.0 copy.9

commit v5 on v4

--- a/solution.py
+++ b/solution.py
@@ -23,8 +23,8 @@
     return ref.at[pl.ds(pl.multiple_of(start, 16), size)]
 
 
-def pair_of(x, y):
-    return (x % 2) * 4 + (y + 2 * (x // 2)) % 4
+def group_of(core, x, y):
+    return core * 4 + (x % 2) * 2 + y % 2
 
 
 def z_offset(n):
@@ -38,12 +38,12 @@
     out,
     signal, rowf, colf, send1, recv1, expand, chan, send2, recv2, gates,
     weave, unweave, blocks, spread_rows,
-    load_sem, own_sem, send_sem, recv1_sem, recv2_sem, block_sem, plane_sem,
+    load_sem, send_sem, recv1_sem, recv2_sem, block_sem, plane_sem,
 ):
     seq, ch = lax.axis_index("seq"), lax.axis_index("ch")
     y, x, core = seq // 32, (seq // 2) % 4, seq % 2
     z = ch * 4 + (seq // 8) % 4
-    mine = pair_of(x, y) * 32 + (x // 2) * 16 + z * 2 + core
+    mine = group_of(core, x, y) * 32 + (x // 2) * 16 + (y // 2) * 8 + z
 
     barrier = pltpu.get_barrier_semaphore()
 
@@ -94,25 +94,26 @@
     pl.semaphore_wait(barrier, 30)
     greet_plane(plane_sem)
 
-    def send_tile(pair, source, target, recv_sem, source_row, own):
+    def send_tile(group, t, source, target, recv_sem, source_row):
+        dst = rows_at(target[0], target[1] * 16, 16)
+
         def body(n, carry):
-            half, far_core = n // 16, (n // 8) % 2
+            far_x = (x + t // 2 % 2 + n // 16 * 2) % 4
+            far_y = (y + t % 2 + n // 8 * 2) % 4
             far_z = (z + z_offset(n % 8)) % 8
-            far_x, far_y = pair // 4 + 2 * half, (pair % 4 + 2 * half) % 4
-            far_seq = far_y * 32 + (far_z % 4) * 8 + far_x * 2 + far_core
+            far_seq = far_y * 32 + (far_z % 4) * 8 + far_x * 2 + group // 4
             far_ch = far_z // 4
-            src = rows_at(source, source_row(half, far_z, far_core) * 16, 16)
+            src = rows_at(source, source_row(far_x // 2, far_y // 2, far_z) * 16, 16)
             is_self = jnp.logical_and(far_seq == seq, far_ch == ch)
 
             @pl.when(is_self)
             def _():
-                pltpu.make_async_copy(src, rows_at(target[0], target[1] * 16, 16), own).start()
+                pltpu.make_async_copy(src, dst, recv_sem).start()
 
             @pl.when(jnp.logical_not(is_self))
             def _():
                 pltpu.make_async_remote_copy(
-                    src_ref=src, dst_ref=rows_at(target[0], target[1] * 16, 16),
-                    send_sem=send_sem, recv_sem=recv_sem,
+                    src_ref=src, dst_ref=dst, send_sem=send_sem, recv_sem=recv_sem,
                     device_id=(far_seq, far_ch), device_id_type=pl.DeviceIdType.MESH,
                 ).start()
 
@@ -121,8 +122,8 @@
         lax.fori_loop(0, 32, body, 0)
 
     def row_step(t, carry):
-        pair = pair_of((x + t // 4) % 4, (y + t % 4) % 4)
-        lanes = pl.ds(pl.multiple_of(pair * 128, 128), 128)
+        group = group_of(t // 4, x + t // 2 % 2, y + t % 2)
+        lanes = pl.ds(pl.multiple_of(group * 128, 128), 128)
 
         @pl.when(t == 0)
         def _():
@@ -139,7 +140,7 @@
             scale = jnp.sum(jnp.where(eye, tw_ref[i:i + 1, lanes], 0.0), axis=1, keepdims=True)
             parts.append((mixed * scale).astype(BF16))
         woven = dot(weave[...], jnp.concatenate(parts, axis=0)).astype(BF16)
-        send1[pl.ds(pl.multiple_of(pair * 512, 512), 512), :] = woven
+        send1[pl.ds(pl.multiple_of(group * 512, 512), 512), :] = woven
 
         @pl.when(t == 0)
         def _():
@@ -147,8 +148,8 @@
             block_copy.start()
 
         send_tile(
-            pair, send1, (recv1, ch * 128 + seq), recv1_sem,
-            lambda half, far_z, far_core: pair * 32 + half * 16 + far_z * 2 + far_core, own_sem.at[0],
+            group, t, send1, (recv1, ch * 128 + seq), recv1_sem,
+            lambda half_x, half_y, far_z: group * 32 + half_x * 16 + half_y * 8 + far_z,
         )
         return carry
 
@@ -164,15 +165,16 @@
 
     lax.fori_loop(0, 64, gate_step, 0)
 
-    def expand_step(pair, carry):
+    def expand_step(group, carry):
         r = iota((256, 512), 0)
-        half = r >> 7
-        far_seq = ((pair % 4 + 2 * half) & 3) * 32 + ((r >> 5) & 3) * 8 + (pair // 4 + 2 * half) * 2 + ((r >> 4) & 1)
+        far_x = group // 2 % 2 + 2 * (r >> 7)
+        far_y = group % 2 + 2 * ((r >> 6) & 1)
+        far_seq = far_y * 32 + ((r >> 4) & 3) * 8 + far_x * 2 + group // 4
         pick = (iota((256, 512), 1) == far_seq * 4 + ((r >> 2) & 3)).astype(F32).astype(BF16)
         taken = lax.dot_general(pick, colf[...], NT, preferred_element_type=F32).astype(BF16)
         widen = (iota((128, 512), 0) == (iota((128, 512), 1) >> 2)).astype(F32).astype(BF16)
         same = (iota((256, 512), 0) & 3) == (iota((256, 512), 1) & 3)
-        rows = pl.ds(pl.multiple_of(pair * 256, 256), 256)
+        rows = pl.ds(pl.multiple_of(group * 256, 256), 256)
         for j in range(4):
             wide = dot(taken[:, j * 128:(j + 1) * 128], widen)
             expand[rows, j * 512:(j + 1) * 512] = jnp.where(same, wide, 0.0).astype(BF16)
@@ -201,44 +203,38 @@
             right = dot(repeat, spread_rows[p0:p0 + 16, :].astype(BF16))
             chan[p0 * 16:p0 * 16 + 256, :] = (left * right).astype(BF16)
 
-    pltpu.make_async_copy(rows_at(recv1, 0, 16), rows_at(recv1, 0, 16), own_sem.at[0]).wait()
-    pltpu.make_async_copy(rows_at(recv1, 0, 255 * 16), rows_at(recv1, 0, 255 * 16), recv1_sem).wait()
+    pltpu.make_async_copy(recv1, recv1, recv1_sem).wait()
 
     def col_step(t, carry):
-        pair = pair_of((x + t // 4) % 4, (y + t % 4) % 4)
-        weights = expand[pl.ds(pl.multiple_of(pair * 256, 256), 256), :]
+        group = group_of((core + t // 4) % 2, x + t // 2 % 2, y + t % 2)
+        weights = expand[pl.ds(pl.multiple_of(group * 256, 256), 256), :]
         low = dot(weights, recv1[0:2048, :]).astype(BF16)
         high = dot(weights, recv1[2048:4096, :]).astype(BF16)
         for h in range(2):
             cut = slice(h * 512, (h + 1) * 512)
             mixed = dot(low, chan[0:512, cut]) + dot(high, chan[512:1024, cut])
-            send2[pl.ds(pl.multiple_of((pair * 2 + h) * 256, 256), 256), :] = mixed.astype(BF16)
+            send2[pl.ds(pl.multiple_of((group * 2 + h) * 256, 256), 256), :] = mixed.astype(BF16)
         send_tile(
-            pair, send2, (recv2, mine), recv2_sem.at[t],
-            lambda half, far_z, far_core: (pair * 2 + far_z // 4) * 16 + half * 8 + (far_z % 4) * 2 + far_core,
-            own_sem.at[1],
+            group, t, send2, (recv2, mine), recv2_sem.at[t],
+            lambda half_x, half_y, far_z: (group * 2 + far_z // 4) * 16 + half_x * 8 + half_y * 4 + far_z % 4,
         )
         return carry
 
     lax.fori_loop(0, 8, col_step, 0)
-    pltpu.make_async_copy(rows_at(recv2, 0, 16), rows_at(recv2, 0, 16), own_sem.at[1]).wait()
-
-    def last_step(t, own):
-        pair = pair_of((x - t // 4 + 4) % 4, (y - t % 4 + 4) % 4)
-        got = rows_at(recv2, pair * 512, 512 - own)
+
+    def last_step(n, carry):
+        t = (n + core * 4) % 8
+        group = group_of(n // 4, x + t // 2 % 2, y + t % 2)
+        got = rows_at(recv2, group * 512, 512)
         pltpu.make_async_copy(got, got, recv2_sem.at[t]).wait()
-        spread = dot(unweave[...], recv2[pl.ds(pl.multiple_of(pair * 512, 512), 512), :])
+        spread = dot(unweave[...], recv2[pl.ds(pl.multiple_of(group * 512, 512), 512), :])
         for i in range(4):
-            part = pl.ds(pl.multiple_of(i * 1024 + pair * 128, 128), 128)
+            part = pl.ds(pl.multiple_of(i * 1024 + group * 128, 128), 128)
             out[part, :] = (signal[part, :].astype(F32) + gates[part, :] * spread[i * 128:(i + 1) * 128, :]).astype(BF16)
 
-    last_step(0, 16)
-
-    def rest(t, carry):
-        last_step(t, 0)
-        return carry
-
-    lax.fori_loop(1, 8, rest, 0)
+        return carry
+
+    lax.fori_loop(0, 8, last_step, 0)
     pltpu.make_async_copy(rows_at(send1, 0, 255 * 16), rows_at(send1, 0, 255 * 16), send_sem).wait()
     pltpu.make_async_copy(rows_at(send2, 0, 255 * 16), rows_at(send2, 0, 255 * 16), send_sem).wait()
 
@@ -268,7 +264,7 @@
             pltpu.VMEM((512, 512), BF16),
             pltpu.VMEM((32, 512), BF16),
             pltpu.VMEM((64, 1024), F32),
-            dma((6,)), dma((2,)), dma, dma, dma((8,)), dma((2,)), pltpu.SemaphoreType.REGULAR,
+            dma((6,)), dma, dma, dma((8,)), dma((2,)), pltpu.SemaphoreType.REGULAR,
         ],
         compiler_params=pltpu.CompilerParams(
             collective_id=0, has_side_effects=True, vmem_limit_bytes=52 << 20),

time: 205 us -> 200 us (0.976)
  Pallas kernels: 200 us -> 196 us
    pallas_call x1, Pallas kernels: 200 us -> 196 us  [per_device(): pl.pallas_call(kernel, out_shape=pltpu.VMEM(signal.shape, signal.dtype),...]
where the time goes in v5:
time: 200 us; the launch traced here: 198 us
  Pallas kernels  196 us (98%)
  local copies, waits for them, and re-layouts  2.02 us (1%)
    pallas_call x1, Pallas kernels, per_device(): pl.pallas_call(kernel, out_shape=pltpu.VMEM(signal.shape, signal.dtype),...  196 us

profile of v5, /device:TPU:38, one launch (start us, length us, event | category | flops | bytes accessed | tf_op | source)
XLA Modules:
  0.0 198.2 jit_solution(12447466590288581223)
XLA Ops:
  0.0 196.2 %shard_map.73 = bf16[4096,512]{1,0:T(8,128)(2,1)S(1)} custom-call(bf16[4096,512]{1,0:T(8,128)(2,1)} %signal_hbm.1, bf16[1024,1024]{1,0:T(8,128)(2,1)} %rowf_hbm.1, bf16[512,512]{1,0:T(8,128)(2,1)} %colf_hbm.1, f32[4,1024]{1,0:T(4,128)} %tw_ref.1, bf16[256,32]{1,0:T(8,128)(2,1)} %bitcast.6, bf16[1024,64]{1,0:T(8,128)(2,1)} %bitcast.5, f32[1,512]{1,0:T(1,128)} %bitcast.7), custom_call_target="tpu_custom_call" | custom-call | tf_op jit(solution)/shard_map/pallas_call | solution.py:247
  196.2 2.0 %copy.9 = bf16[4096,512]{1,0:T(8,128)(2,1)} copy(bf16[4096,512]{1,0:T(8,128)(2,1)S(1)} %shard_map.73) | data formatting | bytes 8388608

commit v6 on v5

--- a/solution.py
+++ b/solution.py
@@ -34,10 +34,10 @@
 
 
 def kernel(
-    signal_hbm, rowf_hbm, colf_hbm, tw_ref, block_ref, mix_ref, gate_ref,
+    signal_hbm, rowf_hbm, colf_hbm, tw_hbm, block_hbm, mix_hbm, gate_hbm,
     out,
     signal, rowf, colf, send1, recv1, expand, chan, send2, recv2, gates,
-    weave, unweave, blocks, spread_rows,
+    weave, unweave, blocks, spread_rows, tw_ref, block_ref, mix_ref, gate_ref, rowf_first, weights,
     load_sem, send_sem, recv1_sem, recv2_sem, block_sem, plane_sem,
 ):
     seq, ch = lax.axis_index("seq"), lax.axis_index("ch")
@@ -65,22 +65,45 @@
         greet(barrier, 0, 0, (n + 1) // 2, (n + 1) % 2)
         return carry
 
+    first = group_of(0, x, y)
+    first_load = pltpu.make_async_copy(
+        rowf_hbm.at[:, pl.ds(pl.multiple_of(first * 128, 128), 128)], rowf_first, load_sem.at[0]
+    )
     loads = []
     for i in range(4):
         part = pl.ds(i * 1024, 1024)
         loads.append(pltpu.make_async_copy(signal_hbm.at[part], signal.at[part], load_sem.at[1 + i]))
-    loads = [pltpu.make_async_copy(rowf_hbm, rowf, load_sem.at[0])] + loads
-    loads.append(pltpu.make_async_copy(colf_hbm, colf, load_sem.at[5]))
+    block_load = pltpu.make_async_copy(block_hbm, block_ref, load_sem.at[5])
+    tw_load = pltpu.make_async_copy(tw_hbm, tw_ref, load_sem.at[6])
+    rowf_load = pltpu.make_async_copy(rowf_hbm, rowf, load_sem.at[7])
+    late_loads = [
+        pltpu.make_async_copy(colf_hbm, colf, load_sem.at[8]),
+        pltpu.make_async_copy(mix_hbm, mix_ref, load_sem.at[9]),
+        pltpu.make_async_copy(gate_hbm, gate_ref, load_sem.at[10]),
+    ]
+    for load in [block_load, first_load, tw_load] + loads:
+        load.start()
     lax.fori_loop(0, 15, greet_line, 0)
     greet_plane(barrier)
-    for load in loads:
+    for load in [rowf_load] + late_loads:
         load.start()
+
+    def answer_line():
+        pl.semaphore_wait(barrier, 30)
+        greet_plane(plane_sem)
+
+    far = z >= 4
+
+    @pl.when(far)
+    def _():
+        answer_line()
 
     o, s = iota((512, 512), 0), iota((512, 512), 1)
     weave[...] = (s == ((o >> 2) & 3) * 128 + (o >> 4) * 4 + (o & 3)).astype(F32).astype(BF16)
     eye = iota((128, 128), 0) == iota((128, 128), 1)
     eye16 = eye.astype(F32).astype(BF16)
 
+    block_load.wait()
     flipped = jnp.zeros((16, 512), F32)
     for q in range(16):
         place = (iota((32, 512), 1) == iota((32, 512), 0) * 16 + q).astype(F32).astype(BF16)
@@ -91,10 +114,8 @@
         send_sem=block_sem.at[0], recv_sem=block_sem.at[1],
         device_id=(seq, 1 - ch), device_id_type=pl.DeviceIdType.MESH,
     )
-    pl.semaphore_wait(barrier, 30)
-    greet_plane(plane_sem)
-
-    def send_tile(group, t, source, target, recv_sem, source_row):
+
+    def send_tile(group, t, source, target, recv_sem, source_row, start=0, stop=32):
         dst = rows_at(target[0], target[1] * 16, 16)
 
         def body(n, carry):
@@ -119,7 +140,7 @@
 
             return carry
 
-        lax.fori_loop(0, 32, body, 0)
+        lax.fori_loop(start, stop, body, 0)
 
     def row_step(t, carry):
         group = group_of(t // 4, x + t // 2 % 2, y + t % 2)
@@ -127,35 +148,58 @@
 
         @pl.when(t == 0)
         def _():
-            loads[0].wait()
-
-        weights = lax.dot_general(eye16, rowf[:, lanes], NT, preferred_element_type=F32).astype(BF16)
+            first_load.wait()
+            tw_load.wait()
+            weights[...] = lax.dot_general(eye16, rowf_first[...], NT, preferred_element_type=F32).astype(BF16)
+
+        @pl.when(t == 1)
+        def _():
+            rowf_load.wait()
+
+        @pl.when(t > 0)
+        def _():
+            weights[...] = lax.dot_general(eye16, rowf[:, lanes], NT, preferred_element_type=F32).astype(BF16)
+
         parts = []
         for i in range(4):
             @pl.when(t == 0)
             def _():
-                loads[1 + i].wait()
-
-            mixed = dot(weights, signal[i * 1024:(i + 1) * 1024, :])
+                loads[i].wait()
+
+            mixed = dot(weights[...], signal[i * 1024:(i + 1) * 1024, :])
             scale = jnp.sum(jnp.where(eye, tw_ref[i:i + 1, lanes], 0.0), axis=1, keepdims=True)
             parts.append((mixed * scale).astype(BF16))
         woven = dot(weave[...], jnp.concatenate(parts, axis=0)).astype(BF16)
         send1[pl.ds(pl.multiple_of(group * 512, 512), 512), :] = woven
 
+        @pl.when(jnp.logical_and(t == 0, jnp.logical_not(far)))
+        def _():
+            answer_line()
+
         @pl.when(t == 0)
         def _():
+            block_copy.start()
+
+        def send_rows(start, stop):
+            send_tile(
+                group, t, send1, (recv1, ch * 128 + seq), recv1_sem,
+                lambda half_x, half_y, far_z: group * 32 + half_x * 16 + half_y * 8 + far_z,
+                start, stop,
+            )
+
+        send_rows(0, 8)
+
+        @pl.when(t == 0)
+        def _():
             pl.semaphore_wait(plane_sem, 15)
-            block_copy.start()
-
-        send_tile(
-            group, t, send1, (recv1, ch * 128 + seq), recv1_sem,
-            lambda half_x, half_y, far_z: group * 32 + half_x * 16 + half_y * 8 + far_z,
-        )
+
+        send_rows(8, 32)
         return carry
 
     lax.fori_loop(0, 8, row_step, 0)
 
-    loads[5].wait()
+    for load in late_loads:
+        load.wait()
 
     def gate_step(n, carry):
         part = pl.ds(pl.multiple_of(n * 64, 64), 64)
@@ -247,7 +291,7 @@
     return pl.pallas_call(
         kernel,
         out_shape=pltpu.VMEM(signal.shape, signal.dtype),
-        in_specs=[anywhere, anywhere, anywhere, inside, inside, inside, inside],
+        in_specs=[anywhere] * 7,
         out_specs=inside,
         scratch_shapes=[
             pltpu.VMEM((4096, 512), BF16),
@@ -264,7 +308,13 @@
             pltpu.VMEM((512, 512), BF16),
             pltpu.VMEM((32, 512), BF16),
             pltpu.VMEM((64, 1024), F32),
-            dma((6,)), dma, dma, dma((8,)), dma((2,)), pltpu.SemaphoreType.REGULAR,
+            pltpu.VMEM((4, 1024), F32),
+            pltpu.VMEM((256, 32), BF16),
+            pltpu.VMEM((1024, 64), BF16),
+            pltpu.VMEM((1, 512), F32),
+            pltpu.VMEM((1024, 128), BF16),
+            pltpu.VMEM((128, 1024), BF16),
+            dma((11,)), dma, dma, dma((8,)), dma((2,)), pltpu.SemaphoreType.REGULAR,
         ],
         compiler_params=pltpu.CompilerParams(
             collective_id=0, has_side_effects=True, vmem_limit_bytes=52 << 20),

time: 200 us -> 198 us (0.990)
  no operation moved by 1% of the time
where the time goes in v6:
time: 198 us
  Pallas kernels  196 us (99%)
  local copies, waits for them, and re-layouts  2.02 us (1%)
    pallas_call x1, Pallas kernels, per_device(): pl.pallas_call(kernel, out_shape=pltpu.VMEM(signal.shape, signal.dtype),...  196 us

profile of v6, /device:TPU:38, one launch (start us, length us, event | category | flops | bytes accessed | tf_op | source)
XLA Modules:
  0.0 198.1 jit_solution(2389356712820960013)
XLA Ops:
  0.0 196.0 %shard_map.73 = bf16[4096,512]{1,0:T(8,128)(2,1)S(1)} custom-call(bf16[4096,512]{1,0:T(8,128)(2,1)} %signal_hbm.1, bf16[1024,1024]{1,0:T(8,128)(2,1)} %rowf_hbm.1, bf16[512,512]{1,0:T(8,128)(2,1)} %colf_hbm.1, f32[4,1024]{1,0:T(4,128)} %tw_hbm.1, bf16[256,32]{1,0:T(8,128)(2,1)} %bitcast.6, bf16[1024,64]{1,0:T(8,128)(2,1)} %bitcast.5, f32[1,512]{1,0:T(1,128)} %bitcast.7), custom_call_target="tpu_custom_call" | custom-call | tf_op jit(solution)/shard_map/pallas_call | solution.py:291
  196.0 2.0 %copy.9 = bf16[4096,512]{1,0:T(8,128)(2,1)} copy(bf16[4096,512]{1,0:T(8,128)(2,1)S(1)} %shard_map.73) | data formatting | bytes 8388608

commit v7 on v6

--- a/solution.py
+++ b/solution.py
@@ -115,32 +115,24 @@
         device_id=(seq, 1 - ch), device_id_type=pl.DeviceIdType.MESH,
     )
 
-    def send_tile(group, t, source, target, recv_sem, source_row, start=0, stop=32):
+    def send_one(group, dx, dy, half_x, half_y, far_z, source, source_row, target, recv_sem):
+        far_x, far_y = (x + dx + half_x * 2) % 4, (y + dy + half_y * 2) % 4
+        far_seq = far_y * 32 + (far_z % 4) * 8 + far_x * 2 + group // 4
+        far_ch = far_z // 4
+        src = rows_at(source, source_row(far_x // 2, far_y // 2) * 16, 16)
         dst = rows_at(target[0], target[1] * 16, 16)
-
-        def body(n, carry):
-            far_x = (x + t // 2 % 2 + n // 16 * 2) % 4
-            far_y = (y + t % 2 + n // 8 * 2) % 4
-            far_z = (z + z_offset(n % 8)) % 8
-            far_seq = far_y * 32 + (far_z % 4) * 8 + far_x * 2 + group // 4
-            far_ch = far_z // 4
-            src = rows_at(source, source_row(far_x // 2, far_y // 2, far_z) * 16, 16)
-            is_self = jnp.logical_and(far_seq == seq, far_ch == ch)
-
-            @pl.when(is_self)
-            def _():
-                pltpu.make_async_copy(src, dst, recv_sem).start()
-
-            @pl.when(jnp.logical_not(is_self))
-            def _():
-                pltpu.make_async_remote_copy(
-                    src_ref=src, dst_ref=dst, send_sem=send_sem, recv_sem=recv_sem,
-                    device_id=(far_seq, far_ch), device_id_type=pl.DeviceIdType.MESH,
-                ).start()
-
-            return carry
-
-        lax.fori_loop(start, stop, body, 0)
+        is_self = jnp.logical_and(far_seq == seq, far_ch == ch)
+
+        @pl.when(is_self)
+        def _():
+            pltpu.make_async_copy(src, dst, recv_sem).start()
+
+        @pl.when(jnp.logical_not(is_self))
+        def _():
+            pltpu.make_async_remote_copy(
+                src_ref=src, dst_ref=dst, send_sem=send_sem, recv_sem=recv_sem,
+                device_id=(far_seq, far_ch), device_id_type=pl.DeviceIdType.MESH,
+            ).start()
 
     def row_step(t, carry):
         group = group_of(t // 4, x + t // 2 % 2, y + t % 2)
@@ -180,20 +172,22 @@
         def _():
             block_copy.start()
 
-        def send_rows(start, stop):
-            send_tile(
-                group, t, send1, (recv1, ch * 128 + seq), recv1_sem,
-                lambda half_x, half_y, far_z: group * 32 + half_x * 16 + half_y * 8 + far_z,
-                start, stop,
+        def send_row(n, carry):
+            far_z = (z + z_offset(n % 8)) % 8
+            send_one(
+                group, t // 2 % 2, t % 2, n // 16, n // 8 % 2, far_z, send1,
+                lambda half_x, half_y: group * 32 + half_x * 16 + half_y * 8 + far_z,
+                (recv1, ch * 128 + seq), recv1_sem,
             )
-
-        send_rows(0, 8)
+            return carry
+
+        lax.fori_loop(0, 8, send_row, 0)
 
         @pl.when(t == 0)
         def _():
             pl.semaphore_wait(plane_sem, 15)
 
-        send_rows(8, 32)
+        lax.fori_loop(8, 32, send_row, 0)
         return carry
 
     lax.fori_loop(0, 8, row_step, 0)
@@ -250,7 +244,7 @@
     pltpu.make_async_copy(recv1, recv1, recv1_sem).wait()
 
     def col_step(t, carry):
-        group = group_of((core + t // 4) % 2, x + t // 2 % 2, y + t % 2)
+        group = group_of((core + t) % 2, x + t // 4, y + t // 2 % 2)
         weights = expand[pl.ds(pl.multiple_of(group * 256, 256), 256), :]
         low = dot(weights, recv1[0:2048, :]).astype(BF16)
         high = dot(weights, recv1[2048:4096, :]).astype(BF16)
@@ -258,17 +252,39 @@
             cut = slice(h * 512, (h + 1) * 512)
             mixed = dot(low, chan[0:512, cut]) + dot(high, chan[512:1024, cut])
             send2[pl.ds(pl.multiple_of((group * 2 + h) * 256, 256), 256), :] = mixed.astype(BF16)
-        send_tile(
-            group, t, send2, (recv2, mine), recv2_sem.at[t],
-            lambda half_x, half_y, far_z: (group * 2 + far_z // 4) * 16 + half_x * 8 + half_y * 4 + far_z % 4,
+
+        @pl.when(t < 6)
+        def _():
+            def body(n, carry):
+                send_col(t, n // 8, (z + z_offset(n % 8)) % 8)
+                return carry
+
+            lax.fori_loop(0, 32, body, 0)
+
+        @pl.when(t == 7)
+        def _():
+            lax.fori_loop(0, 64, send_last, 0)
+
+        return carry
+
+    def send_col(t, quarter, far_z):
+        group = group_of((core + t) % 2, x + t // 4, y + t // 2 % 2)
+        send_one(
+            group, t // 4, t // 2 % 2, quarter // 2, quarter % 2, far_z, send2,
+            lambda half_x, half_y: (group * 2 + far_z // 4) * 16 + half_x * 8 + half_y * 4 + far_z % 4,
+            (recv2, mine), recv2_sem.at[t],
         )
+
+    def send_last(n, carry):
+        m = n // 2
+        send_col(6 + n % 2, m % 16 // 4, m // 16 * 4 + m % 4)
         return carry
 
     lax.fori_loop(0, 8, col_step, 0)
 
     def last_step(n, carry):
-        t = (n + core * 4) % 8
-        group = group_of(n // 4, x + t // 2 % 2, y + t % 2)
+        t = n % 4 * 2 + (core + n // 4) % 2
+        group = group_of(n // 4, x + t // 4, y + t // 2 % 2)
         got = rows_at(recv2, group * 512, 512)
         pltpu.make_async_copy(got, got, recv2_sem.at[t]).wait()
         spread = dot(unweave[...], recv2[pl.ds(pl.multiple_of(group * 512, 512), 512), :])

time: 198 us -> 198 us (level)
  no operation moved by 1% of the time
where the time goes in v7:
time: 198 us
  Pallas kernels  196 us (99%)
  local copies, waits for them, and re-layouts  2.02 us (1%)
    pallas_call x1, Pallas kernels, per_device(): pl.pallas_call(kernel, out_shape=pltpu.VMEM(signal.shape, signal.dtype),...  196 us

profile of v7, /device:TPU:38, one launch (start us, length us, event | category | flops | bytes accessed | tf_op | source)
XLA Modules:
  0.0 197.8 jit_solution(16045030665896104936)
XLA Ops:
  0.0 195.7 %shard_map.73 = bf16[4096,512]{1,0:T(8,128)(2,1)S(1)} custom-call(bf16[4096,512]{1,0:T(8,128)(2,1)} %signal_hbm.1, bf16[1024,1024]{1,0:T(8,128)(2,1)} %rowf_hbm.1, bf16[512,512]{1,0:T(8,128)(2,1)} %colf_hbm.1, f32[4,1024]{1,0:T(4,128)} %tw_hbm.1, bf16[256,32]{1,0:T(8,128)(2,1)} %bitcast.6, bf16[1024,64]{1,0:T(8,128)(2,1)} %bitcast.5, f32[1,512]{1,0:T(1,128)} %bitcast.7), custom_call_target="tpu_custom_call" | custom-call | tf_op jit(solution)/shard_map/pallas_call | solution.py:307
  195.7 2.0 %copy.9 = bf16[4096,512]{1,0:T(8,128)(2,1)} copy(bf16[4096,512]{1,0:T(8,128)(2,1)S(1)} %shard_map.73) | data formatting | bytes 8388608
